TPU v7x, 32 devices: a whole 2x2x4 slice. The times are simulated.
32 devices in a mesh: gx: 4 (over y, x), gy: 8 (over z, core).
Axes of the slice: x: 2, y: 2, z: 4, core: 2. Of those that a mesh axis runs over, the one named last changes fastest.
Arguments:
- basis: float32 [32, 64, 64, 128], P(None, 'gx', 'gy'), may hold values from -21 to 21
- classes: int32 [64, 64, 128], P('gx', 'gy'), may hold values from 0 to 7
- ports: int32 [64, 64, 128], P('gx', 'gy'), may hold values from 0 to 8, as said below
- taps: float32 [8, 42], replicated, may hold values from 0.05 to 0.5
- port_gain: float32 [8], replicated, may hold values from 0.5 to 4
Outputs:
- next_block: float32 [8, 64, 64, 128], P(None, 'gx', 'gy')
- projection: float32 [32, 8], replicated
- triangle: float32 [8, 8], replicated
Inputs may be any that keep to these rules, and one draw needn't show every extreme that they name: `ports`: 0 means the cell belongs to no port; p in 1..8 names port p.
All inputs are finite; a program needn't handle non-finite values.
Results may differ from a plain program's by a relative error of at most 0.00029.
Values sent between devices are 32-bit elements; how exact they have to be, the bound alone decides.
A program may use at most 64 MiB of HBM per device.

v0:
```python
import jax
import jax.numpy as jnp
from jax import lax
from jax.sharding import PartitionSpec as P

COLS = 8
BLOCKS = 4
REACH = 7
MAT = 8
PORTS = 8


def with_halo(block, sides, width):
    for axis, dim in sides:
        count = lax.axis_size(axis)
        forward = [(i, i + 1) for i in range(count - 1)]
        backward = [(target, source) for source, target in forward]
        low = lax.ppermute(
            lax.slice_in_dim(block, block.shape[dim] - width, None, axis=dim), axis, forward
        )
        high = lax.ppermute(lax.slice_in_dim(block, 0, width, axis=dim), axis, backward)
        block = jnp.concatenate([low, block, high], axis=dim)
    return block


def apply_taps(image, source, coefs, dim, axis_pos, length):
    for j in range(2 * REACH):
        offset = j - REACH if j < REACH else j - REACH + 1
        shifted = lax.slice_in_dim(source, REACH + offset, REACH + offset + length, axis=axis_pos)
        image = image - coefs[2 * REACH * dim + j][None] * shifted
    return image


def per_device(basis, classes, ports, taps, port_gain):
    highest = lax.Precision.HIGHEST
    size_x, size_y, size_z = classes.shape
    block = basis[(BLOCKS - 1) * COLS :]
    kinds = jnp.arange(MAT, dtype=jnp.int32)
    onehot = (classes[None] == kinds[:, None, None, None]).astype(jnp.float32)
    coefs = jnp.einsum("mt,mxyz->txyz", taps, onehot, precision=highest)
    gains_full = jnp.concatenate([jnp.zeros((1,), jnp.float32), port_gain])
    port_kinds = jnp.arange(PORTS + 1, dtype=jnp.int32)
    port_hot = (ports[None] == port_kinds[:, None, None, None]).astype(jnp.float32)
    gain_cell = jnp.einsum("p,pxyz->xyz", gains_full, port_hot, precision=highest)
    diag = (
        1.0
        + jnp.einsum("m,mxyz->xyz", jnp.sum(taps, axis=1), onehot, precision=highest)
        + gain_cell
    )
    image = diag[None] * block
    z_padded = jnp.pad(block, ((0, 0), (0, 0), (0, 0), (REACH, REACH)))
    padded = with_halo(block, (("gx", 1), ("gy", 2)), REACH)
    image = apply_taps(image, padded[:, :, REACH : REACH + size_y, :], coefs, 0, 1, size_x)
    image = apply_taps(image, padded[:, REACH : REACH + size_x, :, :], coefs, 1, 2, size_y)
    image = apply_taps(image, z_padded, coefs, 2, 3, size_z)
    total = size_x * size_y * size_z * lax.axis_size("gx") * lax.axis_size("gy")
    basis_flat = basis.reshape(BLOCKS * COLS, -1)
    image_flat = image.reshape(COLS, -1)
    local_qw = jnp.dot(basis_flat, image_flat.T, precision=highest)
    local_ww = jnp.dot(image_flat, image_flat.T, precision=highest)
    local_qq = jnp.dot(basis_flat, basis_flat.T, precision=highest)
    sum_qw, sum_ww, sum_qq = lax.psum((local_qw, local_ww, local_qq), ("gx", "gy"))
    projection = sum_qw / total
    cross = jnp.dot(projection.T, projection, precision=highest)
    inner = jnp.dot(sum_qq / total, projection, precision=highest)
    gram = sum_ww / total - 2.0 * cross + jnp.dot(projection.T, inner, precision=highest)
    remainder = image_flat - jnp.dot(projection.T, basis_flat, precision=highest)
    lower = jnp.linalg.cholesky(gram)
    solved = lax.linalg.triangular_solve(lower, remainder, left_side=True, lower=True)
    return (solved.reshape(COLS, size_x, size_y, size_z), projection, lower.T)


def solution(mesh):
    in_specs = (P(None, "gx", "gy", None), P("gx", "gy", None), P("gx", "gy", None), P(), P())
    out_specs = (P(None, "gx", "gy", None), P(), P())
    return jax.shard_map(
        per_device, mesh=mesh, in_specs=in_specs, out_specs=out_specs, check_vma=False
    )
```

profile of v0, /device:TPU:0, one launch (start us, length us, event | category | flops | bytes accessed | tf_op | source)
XLA Modules:
  0.0 97.1 jit_solution(1307405450240480122)
XLA Ops:
  0.6 1.1 %fusion.106 = (f32[8,7,8,128]{3,2,1,0:T(8,128)S(1)}, f32[8,7,8,128]{3,2,1,0:T(8,128)S(1)}) fusion(f32[32,16,8,128]{3,2,1,0:T(8,128)} %param.5), kind=kLoop, calls=%fused_computation.182 | loop fusion | bytes 917504 | tf_op jit(solution)/shard_map/slice | solution.py:19
  1.8 4.9 %collective-permute-start = (f32[8,7,8,128]{3,0,2,1:T(8,128)S(1)}, f32[8,7,8,128]{3,0,2,1:T(8,128)S(1)}, u32[]{:S(2)}, u32[]{:S(2)}) collective-permute-start(f32[8,7,8,128]{3,0,2,1:T(8,128)S(1)} %copy.54), channel_id=1, source_target_pairs={{0,8},{8,16},{16,24},{1,9},{9,17},{17,25},{2,10},{10,18},{18,26},{... | collective-permute-start | bytes 688136 | tf_op jit(solution)/shard_map/ppermute | solution.py:18
  6.7 1.3 %collective-permute-start.1 = (f32[8,7,8,128]{3,0,2,1:T(8,128)S(1)}, f32[8,7,8,128]{3,0,2,1:T(8,128)S(1)}, u32[]{:S(2)}, u32[]{:S(2)}) collective-permute-start(f32[8,7,8,128]{3,0,2,1:T(8,128)S(1)} %copy.53), channel_id=1, source_target_pairs={{8,0},{16,8},{24,16},{9,1},{17,9},{25,17},{10,2},{18,10},{26,18},{... | collective-permute-start | bytes 688136 | tf_op jit(solution)/shard_map/ppermute | solution.py:21
  8.0 0.9 iota_compare_fusion.1
  9.0 2.3 %convolution_bitcast_fusion = f32[42,16,8,128]{3,0,2,1:T(8,128)S(1)} fusion(f32[8,42]{1,0:T(8,128)S(1)} %copy-done, s32[16,8,128]{2,1,0:T(8,128)} %param.6), kind=kOutput, calls=%fused_computation.17 | convolution fusion | flops 66191360 | bytes 2819392 | tf_op jit(solution)/shard_map/mt,mxyz->txyz/dot_general | solution.py:40
  11.2 1.6 %copy-done.2 = f32[42,16,8,128]{3,0,2,1:T(8,128)} copy-done((f32[42,16,8,128]{3,0,2,1:T(8,128)}, f32[42,16,8,128]{3,0,2,1:T(8,128)S(1)}, u32[]{:S(2)}) %copy-start.2) | copy-done | bytes 2752536
  12.9 0.9 fusion.105
  14.0 0.5 fusion.3
  14.4 0.4 fusion.97
  14.8 0.3 copy.52
  15.1 3.2 %collective-permute-done.1 = f32[8,7,8,128]{3,0,2,1:T(8,128)S(1)} collective-permute-done((f32[8,7,8,128]{3,0,2,1:T(8,128)S(1)}, f32[8,7,8,128]{3,0,2,1:T(8,128)S(1)}, u32[]{:S(2)}, u32[]{:S(2)}) %collective-permute-start.1) | collective-permute-done | bytes 229408 | tf_op jit(solution)/shard_map/ppermute | solution.py:21
  18.6 1.6 %collective-permute-start.2 = (f32[8,30,7,128]{3,0,2,1:T(8,128)S(1)}, f32[8,30,7,128]{3,0,2,1:T(8,128)S(1)}, u32[]{:S(2)}, u32[]{:S(2)}) collective-permute-start(f32[8,30,7,128]{3,0,2,1:T(8,128)S(1)} %get-tuple-element.58), channel_id=1, source_target_pairs={{0,1},{1,2},{2,3},{3,4},{4,5},{5,6},{6,7},{8,9},{9,10},{10,11},{11... | collective-permute-start | bytes 2580488 | tf_op jit(solution)/shard_map/ppermute | solution.py:18
  20.2 1.5 %collective-permute-start.3 = (f32[8,30,7,128]{3,0,2,1:T(8,128)S(1)}, f32[8,30,7,128]{3,0,2,1:T(8,128)S(1)}, u32[]{:S(2)}, u32[]{:S(2)}) collective-permute-start(f32[8,30,7,128]{3,0,2,1:T(8,128)S(1)} %get-tuple-element.59), channel_id=1, source_target_pairs={{1,0},{2,1},{3,2},{4,3},{5,4},{6,5},{7,6},{9,8},{10,9},{11,10},{12... | collective-permute-start | bytes 2580488 | tf_op jit(solution)/shard_map/ppermute | solution.py:21
  21.7 3.4 %convolution_bitcast_fusion.1 = f32[32,32]{1,0:T(8,128)} fusion(f32[32,16,8,128]{3,2,1,0:T(8,128)S(1)} %copy-done.1), kind=kOutput, calls=%fused_computation.32 | convolution fusion | flops 201326592 | bytes 2101248 | tf_op jit(solution)/shard_map/dot_general | solution.py:61
  25.1 1.5 %fusion.103 = (f32[1,16,8,128]{3,0,2,1:T(1,128)S(1)}, f32[1,16,8,128]{3,0,2,1:T(1,128)S(1)}, f32[1,16,8,128]{3,0,2,1:T(1,128)S(1)}, f32[1,16,8,128]{3,0,2,1:T(1,...) fusion(f32[42,16,8,128]{3,0,2,1:T(8,128)S(1)} %copy-done.3), kind=kLoop, calls=%fused_computation.179 | loop fusion | bytes 2490368 | tf_op jit(solution)/shard_map/slice | solution.py:30
  26.7 1.8 %fusion.104 = (f32[1,16,8,128]{3,0,2,1:T(1,128)}, f32[1,16,8,128]{3,0,2,1:T(1,128)}, f32[1,16,8,128]{3,0,2,1:T(1,128)}, f32[1,16,8,128]{3,0,2,1:T(1,128)}, f32[1...) fusion(f32[42,16,8,128]{3,0,2,1:T(8,128)S(1)} %copy-done.3), kind=kLoop, calls=%fused_computation.180 | loop fusion | bytes 2490368 | tf_op jit(solution)/shard_map/slice | solution.py:30
  28.5 1.5 %maximum_maximum_fusion = (f32[8,30,15,128]{3,0,2,1:T(8,128)S(1)}, f32[8,30,15,128]{3,0,2,1:T(8,128)}) fusion(f32[8,7,8,128]{3,0,2,1:T(8,128)S(1)} %collective-permute-done.1, f32[8,16,8,128]{3,0,2,1:T(8,128)S(1)} %copy.52, f32[8,7,8,128]{3,0,2,1:T(8,128)S(1)} %collective-permute-done, f32[8,30,7,128]{3,0,2,1:T(8,128)S(1)} %collective-permute-done.2, ...), kind=kLoop, calls=%fused_computation.18 | loop fusion | flops 2764800 | bytes 6389760 | tf_op jit(solution)/shard_map/concatenate | solution.py:22
  30.0 8.1 %fusion.76 = f32[8,16,8,128]{3,0,2,1:T(8,128)S(1)} fusion(f32[8,16,8,128]{3,0,2,1:T(8,128)S(1)} %copy.52, f32[8,30,15,128]{3,0,2,1:T(8,128)} %get-tuple-element.57, f32[8,30,15,128]{3,0,2,1:T(8,128)S(1)} %get-tuple-element.56, f32[8,7,8,128]{3,0,2,1:T(8,128)S(1)} %collective-permute-done.1, f32[8,7,8,128]{3,0,2,1:T(8,128)S(1)} %collective-permute-done, ...), kind=kLoop, calls=%fused_computation.125 | loop fusion | flops 12976128 | bytes 11665408 | tf_op jit(solution)/shard_map/sub | solution.py:30
  38.2 1.2 %convolution_bitcast_fusion.2 = f32[8,8]{0,1:T(8,128)S(1)} fusion(f32[8,16,8,128]{3,0,2,1:T(8,128)S(1)} %fusion.76), kind=kOutput, calls=%fused_computation.36 | convolution fusion | flops 12582912 | bytes 524544 | tf_op jit(solution)/shard_map/dot_general | solution.py:60
  39.4 2.6 %convolution_bitcast_fusion.3 = f32[32,8]{0,1:T(8,128)S(1)} fusion(f32[8,16,8,128]{3,0,2,1:T(8,128)S(1)} %fusion.76, f32[32,16,8,128]{3,2,1,0:T(8,128)S(1)} %copy-done.1), kind=kOutput, calls=%fused_computation.37 | convolution fusion | flops 50331648 | bytes 2622464 | tf_op jit(solution)/shard_map/dot_general | solution.py:59
  42.0 47.5 %all-reduce.1 = (f32[32,8]{0,1:T(8,128)S(1)}, f32[8,8]{0,1:T(8,128)S(1)}, f32[32,32]{1,0:T(8,128)S(1)}) all-reduce(f32[32,8]{0,1:T(8,128)S(1)} %convolution_bitcast_fusion.3, f32[8,8]{0,1:T(8,128)S(1)} %convolution_bitcast_fusion.2, f32[32,32]{1,0:T(8,128)S(1)} %copy-done.5), channel_id=1, replica_groups=mesh['gx'=4,'gy'=8] {'gx','gy'}, use_global_device_ids=true, to_apply=%region_2.3 | all-reduce | flops 1344 | bytes 10752 | tf_op jit(solution)/shard_map/psum | solution.py:62
  89.5 0.1 fusion.87
  89.6 0.1 fusion.2
  89.7 0.2 convolution_add_fusion
  90.0 0.7 cholesky.16
  90.8 0.6 compare_reduce_fusion
  91.4 0.6 fusion.94
  92.1 0.6 custom-call.6
  92.7 2.2 %convolution_subtract_fusion = f32[8,16384]{1,0:T(8,128)S(1)} fusion(f32[8,16384]{1,0:T(8,128)S(1)} %bitcast.112, f32[32,8]{0,1:T(8,128)S(1)} %broadcast_multiply_fusion, f32[4,8,128,128]{3,2,1,0:T(8,128)S(1)} %bitcast.111), kind=kOutput, calls=%fused_computation | convolution fusion | flops 50462720 | bytes 3146752 | tf_op jit(solution)/shard_map/dot_general | solution.py:67
  95.0 0.6 fusion.90
  95.6 0.9 copy.28
  96.5 0.7 copy.29
  (31 shorter events, 0.7 us)
Async XLA Ops:
  0.6 8.3 %copy-start = (f32[8,42]{1,0:T(8,128)S(1)}, f32[8,42]{1,0:T(8,128)}, u32[]{:S(2)}) copy-start(f32[8,42]{1,0:T(8,128)} %param.8) | copy-start | bytes 4036
  1.8 13.4 %collective-permute-start = (f32[8,7,8,128]{3,0,2,1:T(8,128)S(1)}, f32[8,7,8,128]{3,0,2,1:T(8,128)S(1)}, u32[]{:S(2)}, u32[]{:S(2)}) collective-permute-start(f32[8,7,8,128]{3,0,2,1:T(8,128)S(1)} %copy.54), channel_id=1, source_target_pairs={{0,8},{8,16},{16,24},{1,9},{9,17},{17,25},{2,10},{10,18},{18,26},{... | collective-permute-start | bytes 688136 | tf_op jit(solution)/shard_map/ppermute | solution.py:18
  6.7 7.1 %copy-start.6 = (s32[16,8,128]{2,1,0:T(8,128)S(1)}, s32[16,8,128]{2,1,0:T(8,128)}, u32[]{:S(2)}) copy-start(s32[16,8,128]{2,1,0:T(8,128)} %param.7) | copy-start | bytes 196612
  6.7 7.3 %copy-start.7 = (f32[8]{0:T(128)S(1)}, f32[8]{0:T(128)}, u32[]{:S(2)}) copy-start(f32[8]{0:T(128)} %param.9) | copy-start | bytes 100
  6.7 11.6 %collective-permute-start.1 = (f32[8,7,8,128]{3,0,2,1:T(8,128)S(1)}, f32[8,7,8,128]{3,0,2,1:T(8,128)S(1)}, u32[]{:S(2)}, u32[]{:S(2)}) collective-permute-start(f32[8,7,8,128]{3,0,2,1:T(8,128)S(1)} %copy.53), channel_id=1, source_target_pairs={{8,0},{16,8},{24,16},{9,1},{17,9},{25,17},{10,2},{18,10},{26,18},{... | collective-permute-start | bytes 688136 | tf_op jit(solution)/shard_map/ppermute | solution.py:21
  11.2 1.6 %copy-start.2 = (f32[42,16,8,128]{3,0,2,1:T(8,128)}, f32[42,16,8,128]{3,0,2,1:T(8,128)S(1)}, u32[]{:S(2)}) copy-start(f32[42,16,8,128]{3,0,2,1:T(8,128)S(1)} %convolution_bitcast_fusion) | copy-start | bytes 8257540
  12.9 1.9 %slice-start = ((f32[32,16,8,128]{3,2,1,0:T(8,128)}), f32[8,16,8,128]{3,2,1,0:T(8,128)S(1)}, s32[]{:S(2)}) async-start(f32[32,16,8,128]{3,2,1,0:T(8,128)} %param.5), calls=%async_computation | async-start | bytes 1048576 | tf_op jit(solution)/shard_map/slice | solution.py:37
  18.4 3.2 %copy-start.1 = (f32[32,16,8,128]{3,2,1,0:T(8,128)S(1)}, f32[32,16,8,128]{3,2,1,0:T(8,128)}, u32[]{:S(2)}) copy-start(f32[32,16,8,128]{3,2,1,0:T(8,128)} %param.5) | copy-start | bytes 6291460
  18.4 6.7 %copy-start.3 = (f32[42,16,8,128]{3,0,2,1:T(8,128)S(1)}, f32[42,16,8,128]{3,0,2,1:T(8,128)}, u32[]{:S(2)}) copy-start(f32[42,16,8,128]{3,0,2,1:T(8,128)} %copy-done.2) | copy-start | bytes 8257540
  18.6 9.9 %collective-permute-start.2 = (f32[8,30,7,128]{3,0,2,1:T(8,128)S(1)}, f32[8,30,7,128]{3,0,2,1:T(8,128)S(1)}, u32[]{:S(2)}, u32[]{:S(2)}) collective-permute-start(f32[8,30,7,128]{3,0,2,1:T(8,128)S(1)} %get-tuple-element.58), channel_id=1, source_target_pairs={{0,1},{1,2},{2,3},{3,4},{4,5},{5,6},{6,7},{8,9},{9,10},{10,11},{11... | collective-permute-start | bytes 2580488 | tf_op jit(solution)/shard_map/ppermute | solution.py:18
  20.2 8.3 %collective-permute-start.3 = (f32[8,30,7,128]{3,0,2,1:T(8,128)S(1)}, f32[8,30,7,128]{3,0,2,1:T(8,128)S(1)}, u32[]{:S(2)}, u32[]{:S(2)}) collective-permute-start(f32[8,30,7,128]{3,0,2,1:T(8,128)S(1)} %get-tuple-element.59), channel_id=1, source_target_pairs={{1,0},{2,1},{3,2},{4,3},{5,4},{6,5},{7,6},{9,8},{10,9},{11,10},{12... | collective-permute-start | bytes 2580488 | tf_op jit(solution)/shard_map/ppermute | solution.py:21
  38.1 3.8 %copy-start.5 = (f32[32,32]{1,0:T(8,128)S(1)}, f32[32,32]{1,0:T(8,128)}, u32[]{:S(2)}) copy-start(f32[32,32]{1,0:T(8,128)} %convolution_bitcast_fusion.1) | copy-start | bytes 12292
  89.4 6.1 %copy-start.4 = (f32[32,8]{0,1:T(8,128)}, f32[32,8]{0,1:T(8,128)S(1)}, u32[]{:S(2)}) copy-start(f32[32,8]{0,1:T(8,128)S(1)} %broadcast_multiply_fusion) | copy-start | bytes 3076
where the time goes:
time: 97.5 us; the launch traced here: 97.1 us
  blocking collectives  47.5 us (49%)
  matrix products  13.7 us (14%)
  other arithmetic  13.6 us (14%)
  starting transfers between devices  9.23 us (9%)
  local copies, waits for them, and re-layouts  9.12 us (9%)
  waiting for transfers between devices  3.21 us (3%)
    psum x1, blocking collectives, per_device(): lax.psum((local_qw, local_ww, local_qq), ('gx', 'gy'))  47.5 us
    sub x1, other arithmetic, apply_taps(): image = image - coefs[2 * REACH * dim + j][None] * shifted  8.13 us
    ppermute x2, starting transfers between devices, with_halo(): lax.ppermute(lax.slice_in_dim(block, block.shape[dim] - width, None, axis...  6.46 us
    slice x3, local copies, waits for them, and re-layouts, apply_taps(): image = image - coefs[2 * REACH * dim + j][None] * shifted  4.22 us
    unnamed x21, local copies, waits for them, and re-layouts  3.61 us
    dot_general x1, matrix products, per_device(): local_qq = jnp.dot(basis_flat, basis_flat.T, precision=highest)  3.45 us
    ppermute x2, waiting for transfers between devices, with_halo(): lax.ppermute(lax.slice_in_dim(block, 0, width, axis=dim), axis, backward)  3.2 us
    ppermute x2, starting transfers between devices, with_halo(): lax.ppermute(lax.slice_in_dim(block, 0, width, axis=dim), axis, backward)  2.76 us
  transfers between devices with their start and end apart: 4, of which 1 were waited for; matrix products, arithmetic and copies ran while one was open for 13% of the time, Pallas kernels for 0%

commit v1 on v0

v1 whole, which is shorter than its diff:
```python
import functools

import jax
import jax.numpy as jnp
from jax import lax
from jax.experimental import pallas as pl
from jax.experimental.pallas import tpu as pltpu
from jax.sharding import PartitionSpec as P

COLS = 8
BLOCKS = 4
REACH = 7
MAT = 8
PORTS = 8
GROUP = 4
MESH = pl.DeviceIdType.MESH
NT = (((1,), (1,)), ((), ()))
HIGHEST = lax.Precision.HIGHEST


def offset_of(j):
    return j - REACH if j < REACH else j - REACH + 1


def halves(value):
    high = value.astype(jnp.bfloat16).astype(jnp.float32)
    return jnp.concatenate([high, value - high], axis=0).astype(jnp.bfloat16)


class Exchange:
    def __init__(self, axis, buf, send, recv):
        self.axis, self.buf, self.send, self.recv = axis, buf, send, recv
        self.me, self.count = lax.axis_index(axis), lax.axis_size(axis)

    def copy(self, step, slot, peer):
        return pltpu.make_async_remote_copy(
            src_ref=self.buf.at[slot],
            dst_ref=self.buf.at[slot],
            send_sem=self.send.at[step],
            recv_sem=self.recv.at[slot],
            device_id={self.axis: peer},
            device_id_type=MESH,
        )

    def start(self, value):
        self.buf[self.me] = value

        def body(step, carry):
            self.copy(step, self.me, lax.rem(self.me + step, self.count)).start()
            return carry

        lax.fori_loop(1, self.count, body, 0)

    def finish(self):
        def body(step, carry):
            peer = lax.rem(self.me + step, self.count)
            self.copy(step, peer, peer).wait_recv()
            self.copy(step, self.me, peer).wait_send()
            return carry

        lax.fori_loop(1, self.count, body, 0)
        total = self.buf[0]
        for slot in range(1, self.count):
            total = total + self.buf[slot]
        return total


def kernel(
    total_cells,
    taps_ref,
    gain_ref,
    basis4,
    basis2,
    classes_hbm,
    ports_hbm,
    out2,
    proj_ref,
    tri_ref,
    pad,
    q2,
    qs,
    w2,
    ws,
    coefs,
    diag,
    classes,
    ports,
    qq_y,
    qq_x,
    g_y,
    g_x,
    local_sem,
    block_sem,
    halo_send,
    halo_recv,
    qq_y_send,
    qq_y_recv,
    qq_x_send,
    qq_x_recv,
    g_y_send,
    g_y_recv,
    g_x_send,
    g_x_recv,
):
    size_x, size_y, size_z = classes.shape
    rows = size_x * size_y
    first = (BLOCKS - 1) * COLS
    gx, gy = lax.axis_index("gx"), lax.axis_index("gy")
    nx, ny = lax.axis_size("gx"), lax.axis_size("gy")
    chunks, _, span = qs.shape
    per_chunk = span // size_z

    barrier = pltpu.get_barrier_semaphore()
    for axis, me, count in (("gx", gx, nx), ("gy", gy, ny)):

        def greet(step, carry, axis=axis, me=me, count=count):
            pl.semaphore_signal(
                barrier, inc=1, device_id={axis: lax.rem(me + step, count)}, device_id_type=MESH
            )
            return carry

        lax.fori_loop(1, count, greet, 0)

    load_classes = pltpu.make_async_copy(classes_hbm, classes, local_sem.at[0])
    load_ports = pltpu.make_async_copy(ports_hbm, ports, local_sem.at[1])
    load_basis = pltpu.make_async_copy(basis2, q2, local_sem.at[2])
    load_block = pltpu.make_async_copy(
        basis4.at[pl.ds(first, COLS)],
        pad.at[:, pl.ds(REACH, size_x), pl.ds(size_y, size_y), :],
        block_sem,
    )
    load_classes.start()
    load_ports.start()
    load_block.start()
    load_basis.start()
    pl.semaphore_wait(barrier, nx + ny - 2)

    inner_x, inner_y = pl.ds(REACH, size_x), pl.ds(size_y, size_y)
    ways = (
        ("gy", 1, gy < ny - 1, gy > 0,
         (slice(None), pl.ds(size_y - REACH, REACH)), (inner_x, pl.ds(size_y - REACH, REACH))),
        ("gy", -1, gy > 0, gy < ny - 1,
         (slice(None), pl.ds(0, REACH)), (inner_x, pl.ds(2 * size_y, REACH))),
        ("gx", 1, gx < nx - 1, gx > 0,
         (pl.ds(size_x - REACH, REACH), slice(None)), (pl.ds(0, REACH), inner_y)),
        ("gx", -1, gx > 0, gx < nx - 1,
         (pl.ds(0, REACH), slice(None)), (pl.ds(REACH + size_x, REACH), inner_y)),
    )

    def halo(way, group):
        axis, step, _, _, (from_x, from_y), (to_x, to_y) = ways[way]
        return pltpu.make_async_remote_copy(
            src_ref=basis4.at[pl.ds(first + group * GROUP, GROUP), from_x, from_y, :],
            dst_ref=pad.at[pl.ds(group * GROUP, GROUP), to_x, to_y, :],
            send_sem=halo_send.at[way, group],
            recv_sem=halo_recv.at[way, group],
            device_id={axis: lax.axis_index(axis) + step},
            device_id_type=MESH,
        )

    for group in range(COLS // GROUP):
        for way in range(4):

            @pl.when(ways[way][2])
            def _(way=way, group=group):
                halo(way, group).start()

    for way in range(4):

        @pl.when(jnp.logical_not(ways[way][3]))
        def _(way=way):
            to_x, to_y = ways[way][5]
            pad[:, to_x, to_y, :] = jnp.zeros((COLS, to_x.size, to_y.size, size_z), jnp.float32)

    load_classes.wait()
    load_ports.wait()
    lane = lax.broadcasted_iota(jnp.int32, (size_y, size_z), 1)

    def make_coefs(x, carry):
        kind, port = classes[x], ports[x]
        bits = [(kind & (1 << b)) != 0 for b in range(3)]
        gain = jnp.zeros((size_y, size_z), jnp.float32)
        for p in range(PORTS):
            gain = jnp.where(port == p + 1, gain_ref[p], gain)
        total = 1.0 + gain
        for t in range(6 * REACH):
            level = [taps_ref[m, t] for m in range(MAT)]
            for bit in bits:
                level = [
                    jnp.where(bit, level[2 * i + 1], level[2 * i]) for i in range(len(level) // 2)
                ]
            total = total + level[0]
            value = level[0]
            if t >= 4 * REACH:
                k = offset_of(t - 4 * REACH)
                value = jnp.where((lane + k >= 0) & (lane + k < size_z), value, 0.0)
            coefs[t, x] = value
        diag[x] = total
        return carry

    lax.fori_loop(0, size_x, make_coefs, 0)
    load_block.wait()

    def along_z(x, carry):
        for c in range(COLS):
            own = pad[c, x + REACH, pl.ds(size_y, size_y), :]
            image = diag[x] * own
            for j in range(2 * REACH):
                shifted = pltpu.roll(own, (-offset_of(j)) % size_z, 1)
                image = image - coefs[4 * REACH + j, x] * shifted
            w2[pl.ds(pl.multiple_of(c * rows + x * size_y, size_y), size_y), :] = image
        return carry

    lax.fori_loop(0, size_x, along_z, 0)
    load_basis.wait()

    def gather(ref, count, chunk):
        return jnp.concatenate(
            [
                ref[pl.ds(chunk * per_chunk + i, count, stride=rows), :]
                for i in range(per_chunk)
            ],
            axis=1,
        )

    def own_products(chunk, acc):
        both = halves(gather(q2, BLOCKS * COLS, chunk))
        qs[chunk] = both
        return acc + lax.dot_general(both, both, NT, preferred_element_type=jnp.float32)

    wide = BLOCKS * COLS
    acc = lax.fori_loop(0, chunks, own_products, jnp.zeros((2 * wide, 2 * wide), jnp.float32))
    acc = acc[:wide] + acc[wide:]
    local_qq = acc[:, :wide] + acc[:, wide:]
    fill = jnp.zeros((wide, 128 - wide), jnp.float32)
    exchange = Exchange("gy", qq_y, qq_y_send, qq_y_recv)
    exchange.start(jnp.concatenate([local_qq, fill], axis=1))

    for group in range(COLS // GROUP):
        for way in range(4):

            @pl.when(ways[way][3])
            def _(way=way, group=group):
                halo(way, group).wait_recv()

        def along_xy(x, carry, group=group):
            columns = range(group * GROUP, (group + 1) * GROUP)
            places = [
                pl.ds(pl.multiple_of(c * rows + x * size_y, size_y), size_y) for c in columns
            ]
            images = [w2[place, :] for place in places]
            for j in range(2 * REACH):
                k = offset_of(j)
                coef_x, coef_y = coefs[j, x], coefs[2 * REACH + j, x]
                for i, c in enumerate(columns):
                    images[i] = images[i] - coef_x * pad[c, x + REACH + k, inner_y, :]
                    images[i] = images[i] - coef_y * pad[c, x + REACH, pl.ds(size_y + k, size_y), :]
            for place, image in zip(places, images):
                w2[place, :] = image
            return carry

        lax.fori_loop(0, size_x, along_xy, 0)

    exchange_x = Exchange("gx", qq_x, qq_x_send, qq_x_recv)
    exchange_x.start(exchange.finish())

    def image_products(chunk, acc):
        both = halves(gather(w2, COLS, chunk))
        ws[chunk] = both
        acc_q, acc_w = acc
        acc_q = acc_q + lax.dot_general(both, qs[chunk], NT, preferred_element_type=jnp.float32)
        acc_w = acc_w + lax.dot_general(both, both, NT, preferred_element_type=jnp.float32)
        return acc_q, acc_w

    acc_q, acc_w = lax.fori_loop(
        0,
        chunks,
        image_products,
        (
            jnp.zeros((2 * COLS, 2 * wide), jnp.float32),
            jnp.zeros((2 * COLS, 2 * COLS), jnp.float32),
        ),
    )
    acc_q, acc_w = acc_q[:COLS] + acc_q[COLS:], acc_w[:COLS] + acc_w[COLS:]
    local_g = jnp.concatenate(
        [
            acc_q[:, :wide] + acc_q[:, wide:],
            acc_w[:, :COLS] + acc_w[:, COLS:],
            jnp.zeros((COLS, 128 - wide - COLS), jnp.float32),
        ],
        axis=1,
    )
    g_exchange = Exchange("gy", g_y, g_y_send, g_y_recv)
    g_exchange.start(local_g)
    sum_qq = exchange_x.finish()
    g_exchange_x = Exchange("gx", g_x, g_x_send, g_x_recv)
    g_exchange_x.start(g_exchange.finish())
    sums = g_exchange_x.finish() / total_cells

    proj_t = sums[:, :wide]
    proj_ref[...] = proj_t.T
    row = lax.broadcasted_iota(jnp.int32, (wide, wide), 0)
    column = lax.broadcasted_iota(jnp.int32, (wide, wide), 1)
    middle = jnp.where(row == column, 2.0, 0.0) - sum_qq[:, :wide] / total_cells
    left = jnp.dot(proj_t, middle, precision=HIGHEST, preferred_element_type=jnp.float32)
    gram = sums[:, wide : wide + COLS] - lax.dot_general(
        left, proj_t, NT, precision=HIGHEST, preferred_element_type=jnp.float32
    )
    row = lax.broadcasted_iota(jnp.int32, (COLS, COLS), 0)
    column = lax.broadcasted_iota(jnp.int32, (COLS, COLS), 1)
    eye = jnp.where(row == column, 1.0, 0.0)
    table = jnp.concatenate([-proj_t, eye, gram], axis=1)
    base = wide + COLS
    index = lax.broadcasted_iota(jnp.int32, table.shape, 0)
    for j in range(COLS):
        pivot = table[j : j + 1, :]
        scale = lax.rsqrt(pivot[:, base + j : base + j + 1])
        pivot = pivot * scale
        factor = table[:, base + j : base + j + 1] * scale
        table = jnp.where(index == j, pivot, jnp.where(index > j, table - factor * pivot, table))
    tri_ref[...] = jnp.where(row <= column, table[:, base:], 0.0)

    mix = table[:, :base]
    high = mix.astype(jnp.bfloat16).astype(jnp.float32)
    mix = jnp.concatenate([high, mix - high], axis=0)
    mix = jnp.concatenate([mix[:, :wide], mix[:, :wide]], axis=1), jnp.concatenate(
        [mix[:, wide:], mix[:, wide:]], axis=1
    )
    mix_q, mix_w = mix[0].astype(jnp.bfloat16), mix[1].astype(jnp.bfloat16)

    def combine(chunk, carry):
        result = jnp.dot(mix_q, qs[chunk], preferred_element_type=jnp.float32)
        result = result + jnp.dot(mix_w, ws[chunk], preferred_element_type=jnp.float32)
        result = result[:COLS] + result[COLS:]
        for i in range(per_chunk):
            out2[pl.ds(chunk * per_chunk + i, COLS, stride=rows), :] = result[
                :, i * size_z : (i + 1) * size_z
            ]
        return carry

    lax.fori_loop(0, chunks, combine, 0)
    for group in range(COLS // GROUP):
        for way in range(4):

            @pl.when(ways[way][2])
            def _(way=way, group=group):
                halo(way, group).wait_send()


def per_device(basis, classes, ports, taps, port_gain):
    size_x, size_y, size_z = classes.shape
    rows = size_x * size_y
    wide = BLOCKS * COLS
    nx, ny = lax.axis_size("gx"), lax.axis_size("gy")
    per_chunk = 16 if rows % 16 == 0 else 1
    chunks, span = rows // per_chunk, per_chunk * size_z
    vmem = functools.partial(pltpu.VMEM, dtype=jnp.float32)
    dma = pltpu.SemaphoreType.DMA
    any_space = pl.BlockSpec(memory_space=pl.ANY)
    smem = pl.BlockSpec(memory_space=pltpu.SMEM)
    vmem_spec = pl.BlockSpec(memory_space=pltpu.VMEM)
    groups = COLS // GROUP
    out, projection, triangle = pl.pallas_call(
        functools.partial(kernel, float(rows * size_z * nx * ny)),
        out_shape=(
            jax.ShapeDtypeStruct((COLS * rows, size_z), jnp.float32),
            jax.ShapeDtypeStruct((wide, COLS), jnp.float32),
            jax.ShapeDtypeStruct((COLS, COLS), jnp.float32),
        ),
        in_specs=[smem, smem, any_space, any_space, any_space, any_space],
        out_specs=(vmem_spec, vmem_spec, vmem_spec),
        scratch_shapes=[
            vmem((COLS, size_x + 2 * REACH, 3 * size_y, size_z)),
            vmem((wide * rows, size_z)),
            pltpu.VMEM((chunks, 2 * wide, span), jnp.bfloat16),
            vmem((COLS * rows, size_z)),
            pltpu.VMEM((chunks, 2 * COLS, span), jnp.bfloat16),
            vmem((6 * REACH, size_x, size_y, size_z)),
            vmem((size_x, size_y, size_z)),
            pltpu.VMEM((size_x, size_y, size_z), jnp.int32),
            pltpu.VMEM((size_x, size_y, size_z), jnp.int32),
            vmem((ny, wide, 128)),
            vmem((nx, wide, 128)),
            vmem((ny, COLS, 128)),
            vmem((nx, COLS, 128)),
            dma((3,)),
            dma,
            dma((4, groups)),
            dma((4, groups)),
            dma((ny,)),
            dma((ny,)),
            dma((nx,)),
            dma((nx,)),
            dma((ny,)),
            dma((ny,)),
            dma((nx,)),
            dma((nx,)),
        ],
        compiler_params=pltpu.CompilerParams(
            collective_id=0, has_side_effects=True, vmem_limit_bytes=40 * 1024 * 1024
        ),
    )(taps, port_gain, basis, basis.reshape(wide * rows, size_z), classes, ports)
    return out.reshape(COLS, size_x, size_y, size_z), projection, triangle


def solution(mesh):
    in_specs = (P(None, "gx", "gy", None), P("gx", "gy", None), P("gx", "gy", None), P(), P())
    out_specs = (P(None, "gx", "gy", None), P(), P())
    return jax.shard_map(
        per_device, mesh=mesh, in_specs=in_specs, out_specs=out_specs, check_vma=False
    )
```

time: 97.5 us -> 38.4 us (0.39)
  blocking collectives: 47.5 us -> 0 us
  Pallas kernels: 0 us -> 30.8 us
  matrix products: 13.7 us -> 0 us
  other arithmetic: 13.6 us -> 0 us
  starting transfers between devices: 9.23 us -> 0 us
  waiting for transfers between devices: 3.21 us -> 0 us
  local copies, waits for them, and re-layouts: 9.12 us -> 6.65 us
    psum x1 -> x0, blocking collectives: 47.5 us -> none  [per_device(): lax.psum((local_qw, local_ww, local_qq), ('gx', 'gy'))]
    pallas_call x0 -> x1, Pallas kernels: none -> 30.8 us  [per_device(): pl.pallas_call(functools.partial(kernel, float(rows * size_z * nx * ny)),...]
    dot_general x9 -> x0, matrix products: 12.7 us -> none  [the longest x1 3.45 us: per_device(): local_qq = jnp.dot(basis_flat, basis_flat.T, precision=highest)]
    ppermute x4 -> x0, starting transfers between devices: 9.23 us -> none  [the longest x2 6.46 us: with_halo(): lax.ppermute(lax.slice_in_dim(block, block.shape[dim] - width, None, axis...]
    sub x1 -> x0, other arithmetic: 8.13 us -> none  [apply_taps(): image = image - coefs[2 * REACH * dim + j][None] * shifted]
    slice x7 -> x0, local copies, waits for them, and re-layouts: 5.43 us -> none  [the longest x3 4.22 us: apply_taps(): image = image - coefs[2 * REACH * dim + j][None] * shifted]
    ppermute x4 -> x0, waiting for transfers between devices: 3.21 us -> none  [the longest x2 3.2 us: with_halo(): lax.ppermute(lax.slice_in_dim(block, 0, width, axis=dim), axis, backward)]
    unnamed x21 -> x13, local copies, waits for them, and re-layouts: 3.61 us -> 6.65 us
  transfers between devices with their start and end apart: 4 -> 0, of which waited for: 1 -> 0; matrix products, arithmetic and copies ran while one was open for 13% -> 0% of each run, Pallas kernels for 0% -> 0%
where the time goes in v1:
time: 38.4 us; the launch traced here: 38.1 us
  Pallas kernels  30.8 us (80%)
  local copies, waits for them, and re-layouts  6.65 us (17%)
  between operations  0.65 us (2%)
    pallas_call x1, Pallas kernels, per_device(): pl.pallas_call(functools.partial(kernel, float(rows * size_z * nx * ny)),...  30.8 us
    unnamed x13, local copies, waits for them, and re-layouts  6.65 us

profile of v1, /device:TPU:0, one launch (start us, length us, event | category | flops | bytes accessed | tf_op | source)
XLA Modules:
  0.0 38.1 jit_solution(4298183192099047585)
XLA Ops:
  0.6 0.0 copy-start
  0.6 1.6 %copy-done = f32[32,16,8,128]{3,2,1,0:T(8,128)S(1)} copy-done((f32[32,16,8,128]{3,2,1,0:T(8,128)S(1)}, f32[32,16,8,128]{3,2,1,0:T(8,128)}, u32[]{:S(2)}) %copy-start) | copy-done | bytes 2097176
  2.2 0.0 copy-start.1
  2.2 0.8 %copy-done.1 = s32[16,8,128]{2,1,0:T(8,128)S(1)} copy-done((s32[16,8,128]{2,1,0:T(8,128)S(1)}, s32[16,8,128]{2,1,0:T(8,128)}, u32[]{:S(2)}) %copy-start.1) | copy-done | bytes 65560
  3.1 0.0 copy-start.2
  3.1 0.8 %copy-done.2 = s32[16,8,128]{2,1,0:T(8,128)S(1)} copy-done((s32[16,8,128]{2,1,0:T(8,128)S(1)}, s32[16,8,128]{2,1,0:T(8,128)}, u32[]{:S(2)}) %copy-start.2) | copy-done | bytes 65560
  3.9 0.0 copy-start.3
  3.9 0.7 %copy-done.3 = f32[8,42]{1,0:T(8,128)S(1)} copy-done((f32[8,42]{1,0:T(8,128)S(1)}, f32[8,42]{1,0:T(8,128)}, u32[]{:S(2)}) %copy-start.3) | copy-done | bytes 1368
  4.6 0.0 copy-start.4
  4.6 0.7 %copy-done.4 = f32[8]{0:T(128)S(1)} copy-done((f32[8]{0:T(128)S(1)}, f32[8]{0:T(128)}, u32[]{:S(2)}) %copy-start.4) | copy-done | bytes 56
  5.2 30.8 %shard_map.76 = (f32[1024,128]{1,0:T(8,128)S(1)}, f32[32,8]{1,0:T(8,128)S(1)}, f32[8,8]{1,0:T(8,128)S(1)}) custom-call(f32[8,42]{1,0:T(8,128)S(1)} %copy-done.3, f32[8]{0:T(128)S(1)} %copy-done.4, f32[32,16,8,128]{3,2,1,0:T(8,128)S(1)} %copy-done, f32[4096,128]{1,0:T(8,128)S(1)} %bitcast.2, s32[16,8,128]{2,1,0:T(8,128)S(1)} %copy-done.1, ...), custom_call_target="tpu_custom_call" | custom-call | tf_op jit(solution)/shard_map/pallas_call | solution.py:363
  36.0 0.7 %copy.8 = f32[32,8]{0,1:T(8,128)} copy(f32[32,8]{1,0:T(8,128)S(1)} %get-tuple-element.10) | data formatting | bytes 2048
  36.7 0.8 %copy.11 = f32[8,16,8,128]{3,2,1,0:T(8,128)} copy(f32[8,16,8,128]{3,2,1,0:T(8,128)S(1)} %bitcast.3) | data formatting | bytes 1048576
  37.5 0.6 %copy.12 = f32[8,8]{1,0:T(8,128)} copy(f32[8,8]{1,0:T(8,128)S(1)} %get-tuple-element.17) | data formatting | bytes 512
Async XLA Ops:
  0.6 1.6 %copy-start = (f32[32,16,8,128]{3,2,1,0:T(8,128)S(1)}, f32[32,16,8,128]{3,2,1,0:T(8,128)}, u32[]{:S(2)}) copy-start(f32[32,16,8,128]{3,2,1,0:T(8,128)} %basis4.1) | copy-start | bytes 6291460
  2.2 0.8 %copy-start.1 = (s32[16,8,128]{2,1,0:T(8,128)S(1)}, s32[16,8,128]{2,1,0:T(8,128)}, u32[]{:S(2)}) copy-start(s32[16,8,128]{2,1,0:T(8,128)} %classes_hbm.1) | copy-start | bytes 196612
  3.1 0.8 %copy-start.2 = (s32[16,8,128]{2,1,0:T(8,128)S(1)}, s32[16,8,128]{2,1,0:T(8,128)}, u32[]{:S(2)}) copy-start(s32[16,8,128]{2,1,0:T(8,128)} %ports_hbm.1) | copy-start | bytes 196612
  3.9 0.7 %copy-start.3 = (f32[8,42]{1,0:T(8,128)S(1)}, f32[8,42]{1,0:T(8,128)}, u32[]{:S(2)}) copy-start(f32[8,42]{1,0:T(8,128)} %taps_ref.1) | copy-start | bytes 4036
  4.6 0.7 %copy-start.4 = (f32[8]{0:T(128)S(1)}, f32[8]{0:T(128)}, u32[]{:S(2)}) copy-start(f32[8]{0:T(128)} %gain_ref.1) | copy-start | bytes 100

commit v2 on v1

--- a/solution.py
+++ b/solution.py
@@ -65,17 +65,18 @@
         return total
 
 
-def kernel(
-    total_cells,
-    taps_ref,
-    gain_ref,
+def gather_kernel(
+    taps_hbm,
+    gain_hbm,
     basis4,
     basis2,
     classes_hbm,
     ports_hbm,
-    out2,
-    proj_ref,
-    tri_ref,
+    qs_out,
+    ws_out,
+    sums_out,
+    taps_ref,
+    gain_ref,
     pad,
     q2,
     qs,
@@ -85,6 +86,7 @@
     diag,
     classes,
     ports,
+    sums,
     qq_y,
     qq_x,
     g_y,
@@ -129,6 +131,10 @@
         pad.at[:, pl.ds(REACH, size_x), pl.ds(size_y, size_y), :],
         block_sem,
     )
+    load_taps = pltpu.make_async_copy(taps_hbm, taps_ref, local_sem.at[3])
+    load_gain = pltpu.make_async_copy(gain_hbm, gain_ref, local_sem.at[4])
+    load_taps.start()
+    load_gain.start()
     load_classes.start()
     load_ports.start()
     load_block.start()
@@ -172,6 +178,8 @@
             to_x, to_y = ways[way][5]
             pad[:, to_x, to_y, :] = jnp.zeros((COLS, to_x.size, to_y.size, size_z), jnp.float32)
 
+    load_taps.wait()
+    load_gain.wait()
     load_classes.wait()
     load_ports.wait()
     lane = lax.broadcasted_iota(jnp.int32, (size_y, size_z), 1)
@@ -230,36 +238,42 @@
 
     wide = BLOCKS * COLS
     acc = lax.fori_loop(0, chunks, own_products, jnp.zeros((2 * wide, 2 * wide), jnp.float32))
+    store_qs = pltpu.make_async_copy(qs, qs_out, local_sem.at[5])
+    store_qs.start()
     acc = acc[:wide] + acc[wide:]
     local_qq = acc[:, :wide] + acc[:, wide:]
     fill = jnp.zeros((wide, 128 - wide), jnp.float32)
     exchange = Exchange("gy", qq_y, qq_y_send, qq_y_recv)
     exchange.start(jnp.concatenate([local_qq, fill], axis=1))
 
-    for group in range(COLS // GROUP):
-        for way in range(4):
-
-            @pl.when(ways[way][3])
-            def _(way=way, group=group):
-                halo(way, group).wait_recv()
-
-        def along_xy(x, carry, group=group):
-            columns = range(group * GROUP, (group + 1) * GROUP)
-            places = [
-                pl.ds(pl.multiple_of(c * rows + x * size_y, size_y), size_y) for c in columns
-            ]
-            images = [w2[place, :] for place in places]
-            for j in range(2 * REACH):
-                k = offset_of(j)
-                coef_x, coef_y = coefs[j, x], coefs[2 * REACH + j, x]
-                for i, c in enumerate(columns):
-                    images[i] = images[i] - coef_x * pad[c, x + REACH + k, inner_y, :]
-                    images[i] = images[i] - coef_y * pad[c, x + REACH, pl.ds(size_y + k, size_y), :]
-            for place, image in zip(places, images):
-                w2[place, :] = image
-            return carry
-
-        lax.fori_loop(0, size_x, along_xy, 0)
+    for axis, first_way in (("gy", 0), ("gx", 2)):
+        for group in range(COLS // GROUP):
+            for way in (first_way, first_way + 1):
+
+                @pl.when(ways[way][3])
+                def _(way=way, group=group):
+                    halo(way, group).wait_recv()
+
+            def along(x, carry, axis=axis, group=group):
+                columns = range(group * GROUP, (group + 1) * GROUP)
+                places = [
+                    pl.ds(pl.multiple_of(c * rows + x * size_y, size_y), size_y) for c in columns
+                ]
+                images = [w2[place, :] for place in places]
+                for j in range(2 * REACH):
+                    k = offset_of(j)
+                    if axis == "gx":
+                        coef, at_x, at_y = coefs[j, x], x + REACH + k, inner_y
+                    else:
+                        coef, at_x = coefs[2 * REACH + j, x], x + REACH
+                        at_y = pl.ds(size_y + k, size_y)
+                    for i, c in enumerate(columns):
+                        images[i] = images[i] - coef * pad[c, at_x, at_y, :]
+                for place, image in zip(places, images):
+                    w2[place, :] = image
+                return carry
+
+            lax.fori_loop(0, size_x, along, 0)
 
     exchange_x = Exchange("gx", qq_x, qq_x_send, qq_x_recv)
     exchange_x.start(exchange.finish())
@@ -292,13 +306,60 @@
     )
     g_exchange = Exchange("gy", g_y, g_y_send, g_y_recv)
     g_exchange.start(local_g)
-    sum_qq = exchange_x.finish()
+    store_ws = pltpu.make_async_copy(ws, ws_out, local_sem.at[6])
+    store_ws.start()
+    sums[COLS:, :] = exchange_x.finish()
     g_exchange_x = Exchange("gx", g_x, g_x_send, g_x_recv)
     g_exchange_x.start(g_exchange.finish())
-    sums = g_exchange_x.finish() / total_cells
-
+    sums[:COLS, :] = g_exchange_x.finish()
+    store_sums = pltpu.make_async_copy(sums, sums_out, local_sem.at[7])
+    store_sums.start()
+    for group in range(COLS // GROUP):
+        for way in range(4):
+
+            @pl.when(ways[way][2])
+            def _(way=way, group=group):
+                halo(way, group).wait_send()
+
+    store_qs.wait()
+    store_ws.wait()
+    store_sums.wait()
+
+
+def combine_kernel(
+    total_cells,
+    qs_hbm,
+    ws_hbm,
+    sums_hbm,
+    out_hbm,
+    proj_hbm,
+    tri_hbm,
+    qs,
+    ws,
+    both_sums,
+    out2,
+    proj_ref,
+    tri_ref,
+    qs_sem,
+    ws_sem,
+    small_sem,
+    out_sem,
+):
+    chunks, _, span = qs.shape
+    rows, size_z = out2.shape[0] // COLS, out2.shape[1]
+    per_chunk = span // size_z
+    wide = BLOCKS * COLS
+    load_sums = pltpu.make_async_copy(sums_hbm, both_sums, small_sem.at[0])
+    load_sums.start()
+    load_ws = pltpu.make_async_copy(ws_hbm, ws, ws_sem)
+    load_qs = pltpu.make_async_copy(qs_hbm, qs, qs_sem)
+    load_ws.start()
+    load_qs.start()
+    load_sums.wait()
+    sums = both_sums[:COLS, :] / total_cells
+    sum_qq = both_sums[COLS:, :]
     proj_t = sums[:, :wide]
-    proj_ref[...] = proj_t.T
+    proj_ref[...] = proj_t
     row = lax.broadcasted_iota(jnp.int32, (wide, wide), 0)
     column = lax.broadcasted_iota(jnp.int32, (wide, wide), 1)
     middle = jnp.where(row == column, 2.0, 0.0) - sum_qq[:, :wide] / total_cells
@@ -319,6 +380,10 @@
         factor = table[:, base + j : base + j + 1] * scale
         table = jnp.where(index == j, pivot, jnp.where(index > j, table - factor * pivot, table))
     tri_ref[...] = jnp.where(row <= column, table[:, base:], 0.0)
+    store_proj = pltpu.make_async_copy(proj_ref, proj_hbm, small_sem.at[1])
+    store_tri = pltpu.make_async_copy(tri_ref, tri_hbm, small_sem.at[2])
+    store_proj.start()
+    store_tri.start()
 
     mix = table[:, :base]
     high = mix.astype(jnp.bfloat16).astype(jnp.float32)
@@ -327,6 +392,15 @@
         [mix[:, wide:], mix[:, wide:]], axis=1
     )
     mix_q, mix_w = mix[0].astype(jnp.bfloat16), mix[1].astype(jnp.bfloat16)
+
+    load_ws.wait()
+    load_qs.wait()
+
+    def store(chunk):
+        part = pl.ds(pl.multiple_of(chunk * per_chunk, per_chunk), per_chunk)
+        return pltpu.make_async_copy(
+            out2.reshape(COLS, rows, size_z).at[:, part, :], out_hbm.at[:, part, :], out_sem.at[chunk]
+        )
 
     def combine(chunk, carry):
         result = jnp.dot(mix_q, qs[chunk], preferred_element_type=jnp.float32)
@@ -336,15 +410,18 @@
             out2[pl.ds(chunk * per_chunk + i, COLS, stride=rows), :] = result[
                 :, i * size_z : (i + 1) * size_z
             ]
+        store(chunk).start()
         return carry
 
     lax.fori_loop(0, chunks, combine, 0)
-    for group in range(COLS // GROUP):
-        for way in range(4):
-
-            @pl.when(ways[way][2])
-            def _(way=way, group=group):
-                halo(way, group).wait_send()
+
+    def drain(chunk, carry):
+        store(chunk).wait()
+        return carry
+
+    lax.fori_loop(0, chunks, drain, 0)
+    store_proj.wait()
+    store_tri.wait()
 
 
 def per_device(basis, classes, ports, taps, port_gain):
@@ -356,34 +433,38 @@
     chunks, span = rows // per_chunk, per_chunk * size_z
     vmem = functools.partial(pltpu.VMEM, dtype=jnp.float32)
     dma = pltpu.SemaphoreType.DMA
+    hbm = pl.BlockSpec(memory_space=pltpu.HBM)
     any_space = pl.BlockSpec(memory_space=pl.ANY)
-    smem = pl.BlockSpec(memory_space=pltpu.SMEM)
-    vmem_spec = pl.BlockSpec(memory_space=pltpu.VMEM)
     groups = COLS // GROUP
-    out, projection, triangle = pl.pallas_call(
-        functools.partial(kernel, float(rows * size_z * nx * ny)),
+    qs_shape, ws_shape = (chunks, 2 * wide, span), (chunks, 2 * COLS, span)
+    sums_shape = (COLS + wide, 128)
+    qs, ws, sums = pl.pallas_call(
+        gather_kernel,
         out_shape=(
-            jax.ShapeDtypeStruct((COLS * rows, size_z), jnp.float32),
-            jax.ShapeDtypeStruct((wide, COLS), jnp.float32),
-            jax.ShapeDtypeStruct((COLS, COLS), jnp.float32),
+            jax.ShapeDtypeStruct(qs_shape, jnp.bfloat16),
+            jax.ShapeDtypeStruct(ws_shape, jnp.bfloat16),
+            jax.ShapeDtypeStruct(sums_shape, jnp.float32),
         ),
-        in_specs=[smem, smem, any_space, any_space, any_space, any_space],
-        out_specs=(vmem_spec, vmem_spec, vmem_spec),
+        in_specs=[hbm] * 6,
+        out_specs=(any_space,) * 3,
         scratch_shapes=[
+            pltpu.SMEM(taps.shape, jnp.float32),
+            pltpu.SMEM(port_gain.shape, jnp.float32),
             vmem((COLS, size_x + 2 * REACH, 3 * size_y, size_z)),
             vmem((wide * rows, size_z)),
-            pltpu.VMEM((chunks, 2 * wide, span), jnp.bfloat16),
+            pltpu.VMEM(qs_shape, jnp.bfloat16),
             vmem((COLS * rows, size_z)),
-            pltpu.VMEM((chunks, 2 * COLS, span), jnp.bfloat16),
+            pltpu.VMEM(ws_shape, jnp.bfloat16),
             vmem((6 * REACH, size_x, size_y, size_z)),
             vmem((size_x, size_y, size_z)),
             pltpu.VMEM((size_x, size_y, size_z), jnp.int32),
             pltpu.VMEM((size_x, size_y, size_z), jnp.int32),
+            vmem(sums_shape),
             vmem((ny, wide, 128)),
             vmem((nx, wide, 128)),
             vmem((ny, COLS, 128)),
             vmem((nx, COLS, 128)),
-            dma((3,)),
+            dma((8,)),
             dma,
             dma((4, groups)),
             dma((4, groups)),
@@ -399,8 +480,38 @@
         compiler_params=pltpu.CompilerParams(
             collective_id=0, has_side_effects=True, vmem_limit_bytes=40 * 1024 * 1024
         ),
-    )(taps, port_gain, basis, basis.reshape(wide * rows, size_z), classes, ports)
-    return out.reshape(COLS, size_x, size_y, size_z), projection, triangle
+    )(
+        *(
+            pltpu.with_memory_space_constraint(operand, pltpu.HBM)
+            for operand in (
+                taps, port_gain, basis, basis.reshape(wide * rows, size_z), classes, ports
+            )
+        )
+    )
+    out, projection, triangle = pl.pallas_call(
+        functools.partial(combine_kernel, float(rows * size_z * nx * ny)),
+        out_shape=(
+            jax.ShapeDtypeStruct((COLS, rows, size_z), jnp.float32),
+            jax.ShapeDtypeStruct((COLS, wide), jnp.float32),
+            jax.ShapeDtypeStruct((COLS, COLS), jnp.float32),
+        ),
+        in_specs=[any_space] * 3,
+        out_specs=(hbm,) * 3,
+        scratch_shapes=[
+            pltpu.VMEM(qs_shape, jnp.bfloat16),
+            pltpu.VMEM(ws_shape, jnp.bfloat16),
+            vmem(sums_shape),
+            vmem((COLS * rows, size_z)),
+            vmem((COLS, wide)),
+            vmem((COLS, COLS)),
+            dma,
+            dma,
+            dma((3,)),
+            dma((chunks,)),
+        ],
+        compiler_params=pltpu.CompilerParams(vmem_limit_bytes=24 * 1024 * 1024),
+    )(qs, ws, sums)
+    return out.reshape(COLS, size_x, size_y, size_z), projection.T, triangle
 
 
 def solution(mesh):

time: 38.4 us -> 32.1 us (0.84)
  local copies, waits for them, and re-layouts: 6.65 us -> 0 us
  Pallas kernels: 30.8 us -> 31.4 us
    unnamed x13 -> x0, local copies, waits for them, and re-layouts: 6.65 us -> none
    pallas_call x1 -> x2, Pallas kernels: 30.8 us -> 31.4 us  [the longest x1 27.7 us: per_device(): pl.pallas_call(gather_kernel, out_shape=(jax.ShapeDtypeStruct(qs_shape, j...]
where the time goes in v2:
time: 32.1 us; the launch traced here: 32 us
  Pallas kernels  31.4 us (98%)
  between operations  0.64 us (2%)
    pallas_call x1, Pallas kernels, per_device(): pl.pallas_call(gather_kernel, out_shape=(jax.ShapeDtypeStruct(qs_shape, j...  27.7 us
    pallas_call x1, Pallas kernels, per_device(): pl.pallas_call(functools.partial(combine_kernel, float(rows * size_z * nx...  3.65 us

profile of v2, /device:TPU:0, one launch (start us, length us, event | category | flops | bytes accessed | tf_op | source)
XLA Modules:
  0.0 32.0 jit_solution(4402511105282282738)
XLA Ops:
  0.6 27.7 %shard_map.76 = (bf16[8,64,2048]{2,1,0:T(8,128)(2,1)S(1)}, bf16[8,16,2048]{2,1,0:T(8,128)(2,1)S(1)}, f32[40,128]{1,0:T(8,128)S(1)}) custom-call(f32[8,42]{1,0:T(8,128)} %taps_hbm.1, f32[8]{0:T(128)} %gain_hbm.1, f32[32,16,8,128]{3,2,1,0:T(8,128)} %basis4.1, f32[4096,128]{1,0:T(8,128)} %bitcast.3, s32[16,8,128]{2,1,0:T(8,128)} %classes_hbm.1, ...), custom_call_target="tpu_custom_call" | custom-call | tf_op jit(solution)/shard_map/pallas_call | solution.py:441
  28.3 3.7 %shard_map.77 = (f32[8,128,128]{2,1,0:T(8,128)}, f32[8,32]{1,0:T(8,128)}, f32[8,8]{1,0:T(8,128)}) custom-call(bf16[8,64,2048]{2,1,0:T(8,128)(2,1)S(1)} %get-tuple-element.9.qs_hbm, bf16[8,16,2048]{2,1,0:T(8,128)(2,1)S(1)} %get-tuple-element.10.ws_hbm, f32[40,128]{1,0:T(8,128)S(1)} %get-tuple-element.11.sums_hbm), custom_call_target="tpu_custom_call" | custom-call | tf_op jit(solution)/shard_map/pallas_call | solution.py:491

commit v3 on v2

--- a/solution.py
+++ b/solution.py
@@ -13,6 +13,8 @@
 MAT = 8
 PORTS = 8
 GROUP = 4
+LAYERS = 4
+UNROLL = 4
 MESH = pl.DeviceIdType.MESH
 NT = (((1,), (1,)), ((), ()))
 HIGHEST = lax.Precision.HIGHEST
@@ -72,21 +74,18 @@
     basis2,
     classes_hbm,
     ports_hbm,
-    qs_out,
-    ws_out,
-    sums_out,
+    qs,
+    ws,
+    sums,
     taps_ref,
     gain_ref,
     pad,
     q2,
-    qs,
     w2,
-    ws,
     coefs,
     diag,
     classes,
     ports,
-    sums,
     qq_y,
     qq_x,
     g_y,
@@ -165,7 +164,7 @@
         )
 
     for group in range(COLS // GROUP):
-        for way in range(4):
+        for way in (2, 3, 0, 1):
 
             @pl.when(ways[way][2])
             def _(way=way, group=group):
@@ -182,31 +181,32 @@
     load_gain.wait()
     load_classes.wait()
     load_ports.wait()
-    lane = lax.broadcasted_iota(jnp.int32, (size_y, size_z), 1)
-
-    def make_coefs(x, carry):
-        kind, port = classes[x], ports[x]
+    layers = LAYERS if size_x % LAYERS == 0 else 1
+    lane = lax.broadcasted_iota(jnp.int32, (layers, size_y, size_z), 2)
+
+    def make_coefs(step, carry):
+        place = pl.ds(step * layers, layers)
+        kind, port = classes[place], ports[place]
         bits = [(kind & (1 << b)) != 0 for b in range(3)]
-        gain = jnp.zeros((size_y, size_z), jnp.float32)
+        total = jnp.ones(kind.shape, jnp.float32)
         for p in range(PORTS):
-            gain = jnp.where(port == p + 1, gain_ref[p], gain)
-        total = 1.0 + gain
+            total = jnp.where(port == p + 1, 1.0 + gain_ref[p], total)
         for t in range(6 * REACH):
             level = [taps_ref[m, t] for m in range(MAT)]
             for bit in bits:
                 level = [
                     jnp.where(bit, level[2 * i + 1], level[2 * i]) for i in range(len(level) // 2)
                 ]
-            total = total + level[0]
             value = level[0]
+            total = total + value
             if t >= 4 * REACH:
                 k = offset_of(t - 4 * REACH)
-                value = jnp.where((lane + k >= 0) & (lane + k < size_z), value, 0.0)
-            coefs[t, x] = value
-        diag[x] = total
+                value = jnp.where(lane < -k if k < 0 else lane >= size_z - k, 0.0, value)
+            coefs[t, place] = value
+        diag[place] = total
         return carry
 
-    lax.fori_loop(0, size_x, make_coefs, 0)
+    lax.fori_loop(0, size_x // layers, make_coefs, 0)
     load_block.wait()
 
     def along_z(x, carry):
@@ -237,9 +237,9 @@
         return acc + lax.dot_general(both, both, NT, preferred_element_type=jnp.float32)
 
     wide = BLOCKS * COLS
-    acc = lax.fori_loop(0, chunks, own_products, jnp.zeros((2 * wide, 2 * wide), jnp.float32))
-    store_qs = pltpu.make_async_copy(qs, qs_out, local_sem.at[5])
-    store_qs.start()
+    acc = lax.fori_loop(
+        0, chunks, own_products, jnp.zeros((2 * wide, 2 * wide), jnp.float32), unroll=UNROLL
+    )
     acc = acc[:wide] + acc[wide:]
     local_qq = acc[:, :wide] + acc[:, wide:]
     fill = jnp.zeros((wide, 128 - wide), jnp.float32)
@@ -294,6 +294,7 @@
             jnp.zeros((2 * COLS, 2 * wide), jnp.float32),
             jnp.zeros((2 * COLS, 2 * COLS), jnp.float32),
         ),
+        unroll=UNROLL,
     )
     acc_q, acc_w = acc_q[:COLS] + acc_q[COLS:], acc_w[:COLS] + acc_w[COLS:]
     local_g = jnp.concatenate(
@@ -306,14 +307,10 @@
     )
     g_exchange = Exchange("gy", g_y, g_y_send, g_y_recv)
     g_exchange.start(local_g)
-    store_ws = pltpu.make_async_copy(ws, ws_out, local_sem.at[6])
-    store_ws.start()
     sums[COLS:, :] = exchange_x.finish()
     g_exchange_x = Exchange("gx", g_x, g_x_send, g_x_recv)
     g_exchange_x.start(g_exchange.finish())
     sums[:COLS, :] = g_exchange_x.finish()
-    store_sums = pltpu.make_async_copy(sums, sums_out, local_sem.at[7])
-    store_sums.start()
     for group in range(COLS // GROUP):
         for way in range(4):
 
@@ -321,27 +318,18 @@
             def _(way=way, group=group):
                 halo(way, group).wait_send()
 
-    store_qs.wait()
-    store_ws.wait()
-    store_sums.wait()
-
 
 def combine_kernel(
     total_cells,
-    qs_hbm,
-    ws_hbm,
-    sums_hbm,
+    qs,
+    ws,
+    both_sums,
     out_hbm,
     proj_hbm,
     tri_hbm,
-    qs,
-    ws,
-    both_sums,
     out2,
     proj_ref,
     tri_ref,
-    qs_sem,
-    ws_sem,
     small_sem,
     out_sem,
 ):
@@ -349,13 +337,6 @@
     rows, size_z = out2.shape[0] // COLS, out2.shape[1]
     per_chunk = span // size_z
     wide = BLOCKS * COLS
-    load_sums = pltpu.make_async_copy(sums_hbm, both_sums, small_sem.at[0])
-    load_sums.start()
-    load_ws = pltpu.make_async_copy(ws_hbm, ws, ws_sem)
-    load_qs = pltpu.make_async_copy(qs_hbm, qs, qs_sem)
-    load_ws.start()
-    load_qs.start()
-    load_sums.wait()
     sums = both_sums[:COLS, :] / total_cells
     sum_qq = both_sums[COLS:, :]
     proj_t = sums[:, :wide]
@@ -373,15 +354,15 @@
     table = jnp.concatenate([-proj_t, eye, gram], axis=1)
     base = wide + COLS
     index = lax.broadcasted_iota(jnp.int32, table.shape, 0)
-    for j in range(COLS):
-        pivot = table[j : j + 1, :]
-        scale = lax.rsqrt(pivot[:, base + j : base + j + 1])
-        pivot = pivot * scale
-        factor = table[:, base + j : base + j + 1] * scale
-        table = jnp.where(index == j, pivot, jnp.where(index > j, table - factor * pivot, table))
+    for j in range(COLS - 1):
+        factor = jnp.broadcast_to(table[:, base + j : base + j + 1], table.shape)
+        factor = jnp.where(index > j, factor / factor[j : j + 1, :], 0.0)
+        table = table - factor * table[j : j + 1, :]
+    pivots = jnp.sum(jnp.where(row == column, table[:, base:], 0.0), axis=1, keepdims=True)
+    table = table * lax.rsqrt(pivots)
     tri_ref[...] = jnp.where(row <= column, table[:, base:], 0.0)
-    store_proj = pltpu.make_async_copy(proj_ref, proj_hbm, small_sem.at[1])
-    store_tri = pltpu.make_async_copy(tri_ref, tri_hbm, small_sem.at[2])
+    store_proj = pltpu.make_async_copy(proj_ref, proj_hbm, small_sem.at[0])
+    store_tri = pltpu.make_async_copy(tri_ref, tri_hbm, small_sem.at[1])
     store_proj.start()
     store_tri.start()
 
@@ -392,9 +373,6 @@
         [mix[:, wide:], mix[:, wide:]], axis=1
     )
     mix_q, mix_w = mix[0].astype(jnp.bfloat16), mix[1].astype(jnp.bfloat16)
-
-    load_ws.wait()
-    load_qs.wait()
 
     def store(chunk):
         part = pl.ds(pl.multiple_of(chunk * per_chunk, per_chunk), per_chunk)
@@ -413,7 +391,7 @@
         store(chunk).start()
         return carry
 
-    lax.fori_loop(0, chunks, combine, 0)
+    lax.fori_loop(0, chunks, combine, 0, unroll=UNROLL)
 
     def drain(chunk, carry):
         store(chunk).wait()
@@ -434,7 +412,7 @@
     vmem = functools.partial(pltpu.VMEM, dtype=jnp.float32)
     dma = pltpu.SemaphoreType.DMA
     hbm = pl.BlockSpec(memory_space=pltpu.HBM)
-    any_space = pl.BlockSpec(memory_space=pl.ANY)
+    vmem_spec = pl.BlockSpec(memory_space=pltpu.VMEM)
     groups = COLS // GROUP
     qs_shape, ws_shape = (chunks, 2 * wide, span), (chunks, 2 * COLS, span)
     sums_shape = (COLS + wide, 128)
@@ -446,25 +424,22 @@
             jax.ShapeDtypeStruct(sums_shape, jnp.float32),
         ),
         in_specs=[hbm] * 6,
-        out_specs=(any_space,) * 3,
+        out_specs=(vmem_spec,) * 3,
         scratch_shapes=[
             pltpu.SMEM(taps.shape, jnp.float32),
             pltpu.SMEM(port_gain.shape, jnp.float32),
             vmem((COLS, size_x + 2 * REACH, 3 * size_y, size_z)),
             vmem((wide * rows, size_z)),
-            pltpu.VMEM(qs_shape, jnp.bfloat16),
             vmem((COLS * rows, size_z)),
-            pltpu.VMEM(ws_shape, jnp.bfloat16),
             vmem((6 * REACH, size_x, size_y, size_z)),
             vmem((size_x, size_y, size_z)),
             pltpu.VMEM((size_x, size_y, size_z), jnp.int32),
             pltpu.VMEM((size_x, size_y, size_z), jnp.int32),
-            vmem(sums_shape),
             vmem((ny, wide, 128)),
             vmem((nx, wide, 128)),
             vmem((ny, COLS, 128)),
             vmem((nx, COLS, 128)),
-            dma((8,)),
+            dma((5,)),
             dma,
             dma((4, groups)),
             dma((4, groups)),
@@ -495,18 +470,13 @@
             jax.ShapeDtypeStruct((COLS, wide), jnp.float32),
             jax.ShapeDtypeStruct((COLS, COLS), jnp.float32),
         ),
-        in_specs=[any_space] * 3,
+        in_specs=[vmem_spec] * 3,
         out_specs=(hbm,) * 3,
         scratch_shapes=[
-            pltpu.VMEM(qs_shape, jnp.bfloat16),
-            pltpu.VMEM(ws_shape, jnp.bfloat16),
-            vmem(sums_shape),
             vmem((COLS * rows, size_z)),
             vmem((COLS, wide)),
             vmem((COLS, COLS)),
-            dma,
-            dma,
-            dma((3,)),
+            dma((2,)),
             dma((chunks,)),
         ],
         compiler_params=pltpu.CompilerParams(vmem_limit_bytes=24 * 1024 * 1024),

time: 32.1 us -> 29.4 us (0.916)
  Pallas kernels: 31.4 us -> 28.6 us
    pallas_call x1, Pallas kernels: 27.7 us -> 25.7 us  [per_device(): pl.pallas_call(gather_kernel, out_shape=(jax.ShapeDtypeStruct(qs_shape, j...]
    pallas_call x1, Pallas kernels: 3.65 us -> 2.9 us  [per_device(): pl.pallas_call(functools.partial(combine_kernel, float(rows * size_z * nx...]
where the time goes in v3:
time: 29.4 us; the launch traced here: 29.2 us
  Pallas kernels  28.6 us (97%)
  between operations  0.64 us (2%)
    pallas_call x1, Pallas kernels, per_device(): pl.pallas_call(gather_kernel, out_shape=(jax.ShapeDtypeStruct(qs_shape, j...  25.7 us
    pallas_call x1, Pallas kernels, per_device(): pl.pallas_call(functools.partial(combine_kernel, float(rows * size_z * nx...  2.9 us

profile of v3, /device:TPU:0, one launch (start us, length us, event | category | flops | bytes accessed | tf_op | source)
XLA Modules:
  0.0 29.2 jit_solution(10166438816761319870)
XLA Ops:
  0.6 25.7 %shard_map.76 = (bf16[8,64,2048]{2,1,0:T(8,128)(2,1)S(1)}, bf16[8,16,2048]{2,1,0:T(8,128)(2,1)S(1)}, f32[40,128]{1,0:T(8,128)S(1)}) custom-call(f32[8,42]{1,0:T(8,128)} %taps_hbm.1, f32[8]{0:T(128)} %gain_hbm.1, f32[32,16,8,128]{3,2,1,0:T(8,128)} %basis4.1, f32[4096,128]{1,0:T(8,128)} %bitcast.3, s32[16,8,128]{2,1,0:T(8,128)} %classes_hbm.1, ...), custom_call_target="tpu_custom_call" | custom-call | tf_op jit(solution)/shard_map/pallas_call | solution.py:419
  26.3 2.9 %shard_map.77 = (f32[8,128,128]{2,1,0:T(8,128)}, f32[8,32]{1,0:T(8,128)}, f32[8,8]{1,0:T(8,128)}) custom-call(bf16[8,64,2048]{2,1,0:T(8,128)(2,1)S(1)} %get-tuple-element.9.qs, bf16[8,16,2048]{2,1,0:T(8,128)(2,1)S(1)} %get-tuple-element.10.ws, f32[40,128]{1,0:T(8,128)S(1)} %get-tuple-element.11.both_sums), custom_call_target="tpu_custom_call" | custom-call | tf_op jit(solution)/shard_map/pallas_call | solution.py:466

commit v4 on v3

--- a/solution.py
+++ b/solution.py
@@ -57,7 +57,6 @@
         def body(step, carry):
             peer = lax.rem(self.me + step, self.count)
             self.copy(step, peer, peer).wait_recv()
-            self.copy(step, self.me, peer).wait_send()
             return carry
 
         lax.fori_loop(1, self.count, body, 0)
@@ -66,8 +65,16 @@
             total = total + self.buf[slot]
         return total
 
+    def drain(self):
+        def body(step, carry):
+            self.copy(step, self.me, lax.rem(self.me + step, self.count)).wait_send()
+            return carry
+
+        lax.fori_loop(1, self.count, body, 0)
+
 
 def gather_kernel(
+    row_length,
     taps_hbm,
     gain_hbm,
     basis4,
@@ -86,6 +93,7 @@
     diag,
     classes,
     ports,
+    relay,
     qq_y,
     qq_x,
     g_y,
@@ -94,6 +102,9 @@
     block_sem,
     halo_send,
     halo_recv,
+    relay_send,
+    relay_recv,
+    forward_send,
     qq_y_send,
     qq_y_recv,
     qq_x_send,
@@ -163,10 +174,62 @@
             device_id_type=MESH,
         )
 
+    turns = []
+    if row_length:
+        for last in range(row_length - 1, nx - 1, row_length):
+            corners = (last + 1 - row_length, last + row_length)
+            turns += [(0, last, last + 1, corners), (1, last + 1, last, corners)]
+    turning = [jnp.bool_(False), jnp.bool_(False)]
+    for direction, source, _, _ in turns:
+        turning[direction] = jnp.logical_or(turning[direction], gx == source)
+
+    def to_corner(direction, group, corner):
+        from_x, from_y = ways[2 + direction][4]
+        return pltpu.make_async_remote_copy(
+            src_ref=basis4.at[pl.ds(first + group * GROUP, GROUP), from_x, from_y, :],
+            dst_ref=relay.at[direction],
+            send_sem=relay_send.at[direction, group],
+            recv_sem=relay_recv.at[direction],
+            device_id={"gx": corner},
+            device_id_type=MESH,
+        )
+
+    def from_corner(direction, group, target):
+        to_x, to_y = ways[2 + direction][5]
+        return pltpu.make_async_remote_copy(
+            src_ref=relay.at[direction],
+            dst_ref=pad.at[pl.ds(group * GROUP, GROUP), to_x, to_y, :],
+            send_sem=forward_send.at[direction],
+            recv_sem=halo_recv.at[2 + direction, group],
+            device_id={"gx": target},
+            device_id_type=MESH,
+        )
+
+    def pass_on(early):
+        for direction, _, target, corners in turns:
+            group = direction if not early else 1 - direction
+
+            @pl.when(gx == corners[group])
+            def _(direction=direction, target=target, group=group):
+                to_corner(direction, group, target).wait_recv()
+                from_corner(direction, group, target).start()
+
+    for direction, source, _, corners in turns:
+
+        @pl.when(gx == source)
+        def _(direction=direction, corners=corners):
+            for group in range(2):
+                to_corner(direction, group, corners[group]).start()
+
+    sends = [ways[way][2] for way in range(4)]
+    for direction in range(2):
+        sends[2 + direction] = jnp.logical_and(
+            sends[2 + direction], jnp.logical_not(turning[direction])
+        )
     for group in range(COLS // GROUP):
         for way in (2, 3, 0, 1):
 
-            @pl.when(ways[way][2])
+            @pl.when(sends[way])
             def _(way=way, group=group):
                 halo(way, group).start()
 
@@ -220,6 +283,7 @@
         return carry
 
     lax.fori_loop(0, size_x, along_z, 0)
+    pass_on(True)
     load_basis.wait()
 
     def gather(ref, count, chunk):
@@ -240,6 +304,7 @@
     acc = lax.fori_loop(
         0, chunks, own_products, jnp.zeros((2 * wide, 2 * wide), jnp.float32), unroll=UNROLL
     )
+    pass_on(False)
     acc = acc[:wide] + acc[wide:]
     local_qq = acc[:, :wide] + acc[:, wide:]
     fill = jnp.zeros((wide, 128 - wide), jnp.float32)
@@ -314,9 +379,23 @@
     for group in range(COLS // GROUP):
         for way in range(4):
 
-            @pl.when(ways[way][2])
+            @pl.when(sends[way])
             def _(way=way, group=group):
                 halo(way, group).wait_send()
+
+    for direction, source, target, corners in turns:
+        for group in range(2):
+
+            @pl.when(gx == source)
+            def _(direction=direction, group=group, corner=corners[group]):
+                to_corner(direction, group, corner).wait_send()
+
+            @pl.when(gx == corners[group])
+            def _(direction=direction, group=group, target=target):
+                from_corner(direction, group, target).wait_send()
+
+    for each in (exchange, exchange_x, g_exchange, g_exchange_x):
+        each.drain()
 
 
 def combine_kernel(
@@ -402,7 +481,7 @@
     store_tri.wait()
 
 
-def per_device(basis, classes, ports, taps, port_gain):
+def per_device(row_length, basis, classes, ports, taps, port_gain):
     size_x, size_y, size_z = classes.shape
     rows = size_x * size_y
     wide = BLOCKS * COLS
@@ -417,7 +496,7 @@
     qs_shape, ws_shape = (chunks, 2 * wide, span), (chunks, 2 * COLS, span)
     sums_shape = (COLS + wide, 128)
     qs, ws, sums = pl.pallas_call(
-        gather_kernel,
+        functools.partial(gather_kernel, row_length),
         out_shape=(
             jax.ShapeDtypeStruct(qs_shape, jnp.bfloat16),
             jax.ShapeDtypeStruct(ws_shape, jnp.bfloat16),
@@ -435,6 +514,7 @@
             vmem((size_x, size_y, size_z)),
             pltpu.VMEM((size_x, size_y, size_z), jnp.int32),
             pltpu.VMEM((size_x, size_y, size_z), jnp.int32),
+            vmem((2, GROUP, REACH, size_y, size_z)),
             vmem((ny, wide, 128)),
             vmem((nx, wide, 128)),
             vmem((ny, COLS, 128)),
@@ -443,6 +523,9 @@
             dma,
             dma((4, groups)),
             dma((4, groups)),
+            dma((2, groups)),
+            dma((2,)),
+            dma((2,)),
             dma((ny,)),
             dma((ny,)),
             dma((nx,)),
@@ -484,9 +567,19 @@
     return out.reshape(COLS, size_x, size_y, size_z), projection.T, triangle
 
 
+def length_of_row(mesh):
+    places = [getattr(device, "coords", None) for device in mesh.devices[:, 0]]
+    if None in places:
+        return 0
+    for i in range(1, len(places)):
+        if sum(a != b for a, b in zip(places[i - 1], places[i])) > 1:
+            return i if len(places) % i == 0 else 0
+    return 0
+
+
 def solution(mesh):
     in_specs = (P(None, "gx", "gy", None), P("gx", "gy", None), P("gx", "gy", None), P(), P())
     out_specs = (P(None, "gx", "gy", None), P(), P())
     return jax.shard_map(
-        per_device, mesh=mesh, in_specs=in_specs, out_specs=out_specs, check_vma=False
-    )
+        functools.partial(per_device, length_of_row(mesh)), mesh=mesh, in_specs=in_specs, out_specs=out_specs, check_vma=False
+    )

time: 29.4 us -> 29.2 us (level)
  no operation moved by 1% of the time
where the time goes in v4:
time: 29.2 us; the launch traced here: 29.1 us
  Pallas kernels  28.5 us (98%)
  between operations  0.64 us (2%)
    pallas_call x1, Pallas kernels, per_device(): pl.pallas_call(functools.partial(gather_kernel, row_length), out_shape=(j...  25.5 us
    pallas_call x1, Pallas kernels, per_device(): pl.pallas_call(functools.partial(combine_kernel, float(rows * size_z * nx...  2.9 us

profile of v4, /device:TPU:0, one launch (start us, length us, event | category | flops | bytes accessed | tf_op | source)
XLA Modules:
  0.0 29.1 jit_solution(3691029062794046183)
XLA Ops:
  0.6 25.5 %shard_map.76 = (bf16[8,64,2048]{2,1,0:T(8,128)(2,1)S(1)}, bf16[8,16,2048]{2,1,0:T(8,128)(2,1)S(1)}, f32[40,128]{1,0:T(8,128)S(1)}) custom-call(f32[8,42]{1,0:T(8,128)} %taps_hbm.1, f32[8]{0:T(128)} %gain_hbm.1, f32[32,16,8,128]{3,2,1,0:T(8,128)} %basis4.1, f32[4096,128]{1,0:T(8,128)} %bitcast.3, s32[16,8,128]{2,1,0:T(8,128)} %classes_hbm.1, ...), custom_call_target="tpu_custom_call" | custom-call | tf_op jit(solution)/shard_map/pallas_call | solution.py:498
  26.2 2.9 %shard_map.77 = (f32[8,128,128]{2,1,0:T(8,128)}, f32[8,32]{1,0:T(8,128)}, f32[8,8]{1,0:T(8,128)}) custom-call(bf16[8,64,2048]{2,1,0:T(8,128)(2,1)S(1)} %get-tuple-element.9.qs, bf16[8,16,2048]{2,1,0:T(8,128)(2,1)S(1)} %get-tuple-element.10.ws, f32[40,128]{1,0:T(8,128)S(1)} %get-tuple-element.11.both_sums), custom_call_target="tpu_custom_call" | custom-call | tf_op jit(solution)/shard_map/pallas_call | solution.py:549

commit v5 on v4

--- a/solution.py
+++ b/solution.py
@@ -91,6 +91,8 @@
     w2,
     coefs,
     diag,
+    bands,
+    parts,
     classes,
     ports,
     relay,
@@ -245,7 +247,12 @@
     load_classes.wait()
     load_ports.wait()
     layers = LAYERS if size_x % LAYERS == 0 else 1
-    lane = lax.broadcasted_iota(jnp.int32, (layers, size_y, size_z), 2)
+    z_sums = []
+    for m in range(MAT):
+        z_sum = taps_ref[m, 4 * REACH]
+        for t in range(4 * REACH + 1, 6 * REACH):
+            z_sum = z_sum + taps_ref[m, t]
+        z_sums.append(z_sum)
 
     def make_coefs(step, carry):
         place = pl.ds(step * layers, layers)
@@ -254,35 +261,65 @@
         total = jnp.ones(kind.shape, jnp.float32)
         for p in range(PORTS):
             total = jnp.where(port == p + 1, 1.0 + gain_ref[p], total)
-        for t in range(6 * REACH):
-            level = [taps_ref[m, t] for m in range(MAT)]
+        for t in range(4 * REACH + 1):
+            level = [taps_ref[m, t] for m in range(MAT)] if t < 4 * REACH else z_sums
             for bit in bits:
                 level = [
                     jnp.where(bit, level[2 * i + 1], level[2 * i]) for i in range(len(level) // 2)
                 ]
-            value = level[0]
-            total = total + value
-            if t >= 4 * REACH:
-                k = offset_of(t - 4 * REACH)
-                value = jnp.where(lane < -k if k < 0 else lane >= size_z - k, 0.0, value)
-            coefs[t, place] = value
+            total = total + level[0]
+            if t < 4 * REACH:
+                coefs[t, place] = level[0]
         diag[place] = total
         return carry
 
     lax.fori_loop(0, size_x // layers, make_coefs, 0)
     load_block.wait()
 
-    def along_z(x, carry):
-        for c in range(COLS):
-            own = pad[c, x + REACH, pl.ds(size_y, size_y), :]
-            image = diag[x] * own
+    distance = lax.broadcasted_iota(jnp.int32, (size_z, size_z), 0) - lax.broadcasted_iota(
+        jnp.int32, (size_z, size_z), 1
+    )
+
+    def make_bands(pair, carry):
+        both = []
+        for m in (2 * pair, 2 * pair + 1):
+            band = jnp.zeros((size_z, size_z), jnp.float32)
             for j in range(2 * REACH):
-                shifted = pltpu.roll(own, (-offset_of(j)) % size_z, 1)
-                image = image - coefs[4 * REACH + j, x] * shifted
-            w2[pl.ds(pl.multiple_of(c * rows + x * size_y, size_y), size_y), :] = image
+                band = jnp.where(distance == offset_of(j), taps_ref[m, 4 * REACH + j], band)
+            both.append(band)
+        band = jnp.concatenate(both, axis=1)
+        high = band.astype(jnp.bfloat16).astype(jnp.float32)
+        bands[pair] = jnp.concatenate([high, high, band - high], axis=0).astype(jnp.bfloat16)
         return carry
 
-    lax.fori_loop(0, size_x, along_z, 0)
+    lax.fori_loop(0, MAT // 2, make_bands, 0)
+
+    def split_block(c, carry):
+        place = pl.ds(pl.multiple_of(c * rows, rows), rows)
+        own = pad[c, inner_x, inner_y, :]
+        w2[place, :] = (diag[...] * own).reshape(rows, size_z)
+        own = own.reshape(rows, size_z)
+        high = own.astype(jnp.bfloat16).astype(jnp.float32)
+        parts[place, :] = jnp.concatenate([high, own - high, high], axis=1).astype(jnp.bfloat16)
+        return carry
+
+    lax.fori_loop(0, COLS, split_block, 0)
+
+    def along_z(pair, carry):
+        kind = classes[...].reshape(rows, size_z)
+        even, odd = kind == 2 * pair, kind == 2 * pair + 1
+        for group in range(COLS // GROUP):
+            lines = pl.ds(group * GROUP * rows, GROUP * rows)
+            result = jnp.dot(parts[lines, :], bands[pair], preferred_element_type=jnp.float32)
+            for i in range(GROUP):
+                place = pl.ds((group * GROUP + i) * rows, rows)
+                mine = result[i * rows : (i + 1) * rows]
+                w2[place, :] -= jnp.where(
+                    even, mine[:, :size_z], jnp.where(odd, mine[:, size_z:], 0.0)
+                )
+        return carry
+
+    lax.fori_loop(0, MAT // 2, along_z, 0)
     pass_on(True)
     load_basis.wait()
 
@@ -510,8 +547,10 @@
             vmem((COLS, size_x + 2 * REACH, 3 * size_y, size_z)),
             vmem((wide * rows, size_z)),
             vmem((COLS * rows, size_z)),
-            vmem((6 * REACH, size_x, size_y, size_z)),
+            vmem((4 * REACH, size_x, size_y, size_z)),
             vmem((size_x, size_y, size_z)),
+            pltpu.VMEM((MAT // 2, 3 * size_z, 2 * size_z), jnp.bfloat16),
+            pltpu.VMEM((COLS * rows, 3 * size_z), jnp.bfloat16),
             pltpu.VMEM((size_x, size_y, size_z), jnp.int32),
             pltpu.VMEM((size_x, size_y, size_z), jnp.int32),
             vmem((2, GROUP, REACH, size_y, size_z)),

time: 29.2 us -> 28.9 us (0.990)
  Pallas kernels: 28.5 us -> 28.1 us
    pallas_call x1, Pallas kernels: 25.5 us -> 25.2 us  [per_device(): pl.pallas_call(functools.partial(gather_kernel, row_length), out_shape=(j...]
where the time goes in v5:
time: 28.9 us; the launch traced here: 28.7 us
  Pallas kernels  28.1 us (97%)
  between operations  0.64 us (2%)
    pallas_call x1, Pallas kernels, per_device(): pl.pallas_call(functools.partial(gather_kernel, row_length), out_shape=(j...  25.2 us
    pallas_call x1, Pallas kernels, per_device(): pl.pallas_call(functools.partial(combine_kernel, float(rows * size_z * nx...  2.9 us

profile of v5, /device:TPU:0, one launch (start us, length us, event | category | flops | bytes accessed | tf_op | source)
XLA Modules:
  0.0 28.7 jit_solution(16121255464635868856)
XLA Ops:
  0.6 25.2 %shard_map.76 = (bf16[8,64,2048]{2,1,0:T(8,128)(2,1)S(1)}, bf16[8,16,2048]{2,1,0:T(8,128)(2,1)S(1)}, f32[40,128]{1,0:T(8,128)S(1)}) custom-call(f32[8,42]{1,0:T(8,128)} %taps_hbm.1, f32[8]{0:T(128)} %gain_hbm.1, f32[32,16,8,128]{3,2,1,0:T(8,128)} %basis4.1, f32[4096,128]{1,0:T(8,128)} %bitcast.3, s32[16,8,128]{2,1,0:T(8,128)} %classes_hbm.1, ...), custom_call_target="tpu_custom_call" | custom-call | tf_op jit(solution)/shard_map/pallas_call | solution.py:535
  25.8 2.9 %shard_map.77 = (f32[8,128,128]{2,1,0:T(8,128)}, f32[8,32]{1,0:T(8,128)}, f32[8,8]{1,0:T(8,128)}) custom-call(bf16[8,64,2048]{2,1,0:T(8,128)(2,1)S(1)} %get-tuple-element.9.qs, bf16[8,16,2048]{2,1,0:T(8,128)(2,1)S(1)} %get-tuple-element.10.ws, f32[40,128]{1,0:T(8,128)S(1)} %get-tuple-element.11.both_sums), custom_call_target="tpu_custom_call" | custom-call | tf_op jit(solution)/shard_map/pallas_call | solution.py:588

commit v6 on v5

--- a/solution.py
+++ b/solution.py
@@ -81,8 +81,7 @@
     basis2,
     classes_hbm,
     ports_hbm,
-    qs,
-    ws,
+    halved,
     sums,
     taps_ref,
     gain_ref,
@@ -121,7 +120,7 @@
     first = (BLOCKS - 1) * COLS
     gx, gy = lax.axis_index("gx"), lax.axis_index("gy")
     nx, ny = lax.axis_size("gx"), lax.axis_size("gy")
-    chunks, _, span = qs.shape
+    chunks, _, span = halved.shape
     per_chunk = span // size_z
 
     barrier = pltpu.get_barrier_semaphore()
@@ -176,62 +175,52 @@
             device_id_type=MESH,
         )
 
+    relayed = COLS // GROUP - 1
     turns = []
     if row_length:
         for last in range(row_length - 1, nx - 1, row_length):
-            corners = (last + 1 - row_length, last + row_length)
-            turns += [(0, last, last + 1, corners), (1, last + 1, last, corners)]
+            turns += [(0, last, last + 1, last + row_length), (1, last + 1, last, last + 1 - row_length)]
     turning = [jnp.bool_(False), jnp.bool_(False)]
     for direction, source, _, _ in turns:
         turning[direction] = jnp.logical_or(turning[direction], gx == source)
 
-    def to_corner(direction, group, corner):
+    def to_corner(direction, corner):
         from_x, from_y = ways[2 + direction][4]
         return pltpu.make_async_remote_copy(
-            src_ref=basis4.at[pl.ds(first + group * GROUP, GROUP), from_x, from_y, :],
+            src_ref=basis4.at[pl.ds(first + relayed * GROUP, GROUP), from_x, from_y, :],
             dst_ref=relay.at[direction],
-            send_sem=relay_send.at[direction, group],
+            send_sem=relay_send.at[direction],
             recv_sem=relay_recv.at[direction],
             device_id={"gx": corner},
             device_id_type=MESH,
         )
 
-    def from_corner(direction, group, target):
+    def from_corner(direction, target):
         to_x, to_y = ways[2 + direction][5]
         return pltpu.make_async_remote_copy(
             src_ref=relay.at[direction],
-            dst_ref=pad.at[pl.ds(group * GROUP, GROUP), to_x, to_y, :],
+            dst_ref=pad.at[pl.ds(relayed * GROUP, GROUP), to_x, to_y, :],
             send_sem=forward_send.at[direction],
-            recv_sem=halo_recv.at[2 + direction, group],
+            recv_sem=halo_recv.at[2 + direction, relayed],
             device_id={"gx": target},
             device_id_type=MESH,
         )
 
-    def pass_on(early):
-        for direction, _, target, corners in turns:
-            group = direction if not early else 1 - direction
-
-            @pl.when(gx == corners[group])
-            def _(direction=direction, target=target, group=group):
-                to_corner(direction, group, target).wait_recv()
-                from_corner(direction, group, target).start()
-
-    for direction, source, _, corners in turns:
+    for direction, source, _, corner in turns:
 
         @pl.when(gx == source)
-        def _(direction=direction, corners=corners):
-            for group in range(2):
-                to_corner(direction, group, corners[group]).start()
-
-    sends = [ways[way][2] for way in range(4)]
-    for direction in range(2):
-        sends[2 + direction] = jnp.logical_and(
-            sends[2 + direction], jnp.logical_not(turning[direction])
-        )
+        def _(direction=direction, corner=corner):
+            to_corner(direction, corner).start()
+
+    def sends(way, group):
+        if way < 2 or group != relayed:
+            return ways[way][2]
+        return jnp.logical_and(ways[way][2], jnp.logical_not(turning[way - 2]))
+
     for group in range(COLS // GROUP):
         for way in (2, 3, 0, 1):
 
-            @pl.when(sends[way])
+            @pl.when(sends(way, group))
             def _(way=way, group=group):
                 halo(way, group).start()
 
@@ -320,7 +309,13 @@
         return carry
 
     lax.fori_loop(0, MAT // 2, along_z, 0)
-    pass_on(True)
+    for direction, _, target, corner in turns:
+
+        @pl.when(gx == corner)
+        def _(direction=direction, target=target):
+            to_corner(direction, target).wait_recv()
+            from_corner(direction, target).start()
+
     load_basis.wait()
 
     def gather(ref, count, chunk):
@@ -334,14 +329,13 @@
 
     def own_products(chunk, acc):
         both = halves(gather(q2, BLOCKS * COLS, chunk))
-        qs[chunk] = both
+        halved[chunk, : 2 * wide, :] = both
         return acc + lax.dot_general(both, both, NT, preferred_element_type=jnp.float32)
 
     wide = BLOCKS * COLS
     acc = lax.fori_loop(
         0, chunks, own_products, jnp.zeros((2 * wide, 2 * wide), jnp.float32), unroll=UNROLL
     )
-    pass_on(False)
     acc = acc[:wide] + acc[wide:]
     local_qq = acc[:, :wide] + acc[:, wide:]
     fill = jnp.zeros((wide, 128 - wide), jnp.float32)
@@ -382,31 +376,25 @@
 
     def image_products(chunk, acc):
         both = halves(gather(w2, COLS, chunk))
-        ws[chunk] = both
-        acc_q, acc_w = acc
-        acc_q = acc_q + lax.dot_general(both, qs[chunk], NT, preferred_element_type=jnp.float32)
-        acc_w = acc_w + lax.dot_general(both, both, NT, preferred_element_type=jnp.float32)
-        return acc_q, acc_w
-
-    acc_q, acc_w = lax.fori_loop(
+        halved[chunk, 2 * wide :, :] = both
+        return acc + lax.dot_general(halved[chunk], both, NT, preferred_element_type=jnp.float32)
+
+    acc = lax.fori_loop(
         0,
         chunks,
         image_products,
-        (
-            jnp.zeros((2 * COLS, 2 * wide), jnp.float32),
-            jnp.zeros((2 * COLS, 2 * COLS), jnp.float32),
-        ),
+        jnp.zeros((2 * (wide + COLS), 2 * COLS), jnp.float32),
         unroll=UNROLL,
     )
-    acc_q, acc_w = acc_q[:COLS] + acc_q[COLS:], acc_w[:COLS] + acc_w[COLS:]
+    acc = acc[:, :COLS] + acc[:, COLS:]
     local_g = jnp.concatenate(
         [
-            acc_q[:, :wide] + acc_q[:, wide:],
-            acc_w[:, :COLS] + acc_w[:, COLS:],
-            jnp.zeros((COLS, 128 - wide - COLS), jnp.float32),
+            acc[:wide] + acc[wide : 2 * wide],
+            acc[2 * wide : 2 * wide + COLS] + acc[2 * wide + COLS :],
+            jnp.zeros((128 - wide - COLS, COLS), jnp.float32),
         ],
-        axis=1,
-    )
+        axis=0,
+    ).T
     g_exchange = Exchange("gy", g_y, g_y_send, g_y_recv)
     g_exchange.start(local_g)
     sums[COLS:, :] = exchange_x.finish()
@@ -416,20 +404,19 @@
     for group in range(COLS // GROUP):
         for way in range(4):
 
-            @pl.when(sends[way])
+            @pl.when(sends(way, group))
             def _(way=way, group=group):
                 halo(way, group).wait_send()
 
-    for direction, source, target, corners in turns:
-        for group in range(2):
-
-            @pl.when(gx == source)
-            def _(direction=direction, group=group, corner=corners[group]):
-                to_corner(direction, group, corner).wait_send()
-
-            @pl.when(gx == corners[group])
-            def _(direction=direction, group=group, target=target):
-                from_corner(direction, group, target).wait_send()
+    for direction, source, target, corner in turns:
+
+        @pl.when(gx == source)
+        def _(direction=direction, corner=corner):
+            to_corner(direction, corner).wait_send()
+
+        @pl.when(gx == corner)
+        def _(direction=direction, target=target):
+            from_corner(direction, target).wait_send()
 
     for each in (exchange, exchange_x, g_exchange, g_exchange_x):
         each.drain()
@@ -437,8 +424,7 @@
 
 def combine_kernel(
     total_cells,
-    qs,
-    ws,
+    halved,
     both_sums,
     out_hbm,
     proj_hbm,
@@ -449,7 +435,7 @@
     small_sem,
     out_sem,
 ):
-    chunks, _, span = qs.shape
+    chunks, _, span = halved.shape
     rows, size_z = out2.shape[0] // COLS, out2.shape[1]
     per_chunk = span // size_z
     wide = BLOCKS * COLS
@@ -485,10 +471,8 @@
     mix = table[:, :base]
     high = mix.astype(jnp.bfloat16).astype(jnp.float32)
     mix = jnp.concatenate([high, mix - high], axis=0)
-    mix = jnp.concatenate([mix[:, :wide], mix[:, :wide]], axis=1), jnp.concatenate(
-        [mix[:, wide:], mix[:, wide:]], axis=1
-    )
-    mix_q, mix_w = mix[0].astype(jnp.bfloat16), mix[1].astype(jnp.bfloat16)
+    mix_q, mix_w = mix[:, :wide], mix[:, wide:]
+    mix = jnp.concatenate([mix_q, mix_q, mix_w, mix_w], axis=1).astype(jnp.bfloat16)
 
     def store(chunk):
         part = pl.ds(pl.multiple_of(chunk * per_chunk, per_chunk), per_chunk)
@@ -497,8 +481,7 @@
         )
 
     def combine(chunk, carry):
-        result = jnp.dot(mix_q, qs[chunk], preferred_element_type=jnp.float32)
-        result = result + jnp.dot(mix_w, ws[chunk], preferred_element_type=jnp.float32)
+        result = jnp.dot(mix, halved[chunk], preferred_element_type=jnp.float32)
         result = result[:COLS] + result[COLS:]
         for i in range(per_chunk):
             out2[pl.ds(chunk * per_chunk + i, COLS, stride=rows), :] = result[
@@ -530,17 +513,16 @@
     hbm = pl.BlockSpec(memory_space=pltpu.HBM)
     vmem_spec = pl.BlockSpec(memory_space=pltpu.VMEM)
     groups = COLS // GROUP
-    qs_shape, ws_shape = (chunks, 2 * wide, span), (chunks, 2 * COLS, span)
+    halved_shape = (chunks, 2 * (wide + COLS), span)
     sums_shape = (COLS + wide, 128)
-    qs, ws, sums = pl.pallas_call(
+    halved, sums = pl.pallas_call(
         functools.partial(gather_kernel, row_length),
         out_shape=(
-            jax.ShapeDtypeStruct(qs_shape, jnp.bfloat16),
-            jax.ShapeDtypeStruct(ws_shape, jnp.bfloat16),
+            jax.ShapeDtypeStruct(halved_shape, jnp.bfloat16),
             jax.ShapeDtypeStruct(sums_shape, jnp.float32),
         ),
         in_specs=[hbm] * 6,
-        out_specs=(vmem_spec,) * 3,
+        out_specs=(vmem_spec,) * 2,
         scratch_shapes=[
             pltpu.SMEM(taps.shape, jnp.float32),
             pltpu.SMEM(port_gain.shape, jnp.float32),
@@ -562,7 +544,7 @@
             dma,
             dma((4, groups)),
             dma((4, groups)),
-            dma((2, groups)),
+            dma((2,)),
             dma((2,)),
             dma((2,)),
             dma((ny,)),
@@ -592,7 +574,7 @@
             jax.ShapeDtypeStruct((COLS, wide), jnp.float32),
             jax.ShapeDtypeStruct((COLS, COLS), jnp.float32),
         ),
-        in_specs=[vmem_spec] * 3,
+        in_specs=[vmem_spec] * 2,
         out_specs=(hbm,) * 3,
         scratch_shapes=[
             vmem((COLS * rows, size_z)),
@@ -602,7 +584,7 @@
             dma((chunks,)),
         ],
         compiler_params=pltpu.CompilerParams(vmem_limit_bytes=24 * 1024 * 1024),
-    )(qs, ws, sums)
+    )(halved, sums)
     return out.reshape(COLS, size_x, size_y, size_z), projection.T, triangle
 
 

time: 28.9 us -> 28.8 us (level)
  no operation moved by 1% of the time
where the time goes in v6:
time: 28.8 us; the launch traced here: 28.7 us
  Pallas kernels  28 us (97%)
  between operations  0.64 us (2%)
    pallas_call x1, Pallas kernels, per_device(): pl.pallas_call(functools.partial(gather_kernel, row_length), out_shape=(j...  25.3 us
    pallas_call x1, Pallas kernels, per_device(): pl.pallas_call(functools.partial(combine_kernel, float(rows * size_z * nx...  2.77 us

profile of v6, /device:TPU:0, one launch (start us, length us, event | category | flops | bytes accessed | tf_op | source)
XLA Modules:
  0.0 28.7 jit_solution(13220636585455143466)
XLA Ops:
  0.6 25.3 %shard_map.76 = (bf16[8,80,2048]{2,1,0:T(8,128)(2,1)S(1)}, f32[40,128]{1,0:T(8,128)S(1)}) custom-call(f32[8,42]{1,0:T(8,128)} %taps_hbm.1, f32[8]{0:T(128)} %gain_hbm.1, f32[32,16,8,128]{3,2,1,0:T(8,128)} %basis4.1, f32[4096,128]{1,0:T(8,128)} %bitcast.3, s32[16,8,128]{2,1,0:T(8,128)} %classes_hbm.1, s32[16,8,128]{2,1,0:T(8,128)} %ports_hbm.1), custom_call_target="tpu_custom_call" | custom-call | tf_op jit(solution)/shard_map/pallas_call | solution.py:518
  25.9 2.8 %shard_map.77 = (f32[8,128,128]{2,1,0:T(8,128)}, f32[8,32]{1,0:T(8,128)}, f32[8,8]{1,0:T(8,128)}) custom-call(bf16[8,80,2048]{2,1,0:T(8,128)(2,1)S(1)} %get-tuple-element.8.halved, f32[40,128]{1,0:T(8,128)S(1)} %get-tuple-element.9.both_sums), custom_call_target="tpu_custom_call" | custom-call | tf_op jit(solution)/shard_map/pallas_call | solution.py:570

commit v7 on v6

--- a/solution.py
+++ b/solution.py
@@ -15,6 +15,7 @@
 GROUP = 4
 LAYERS = 4
 UNROLL = 4
+PITCH = 8
 MESH = pl.DeviceIdType.MESH
 NT = (((1,), (1,)), ((), ()))
 HIGHEST = lax.Precision.HIGHEST
@@ -117,6 +118,7 @@
 ):
     size_x, size_y, size_z = classes.shape
     rows = size_x * size_y
+    pitch = rows + PITCH
     first = (BLOCKS - 1) * COLS
     gx, gy = lax.axis_index("gx"), lax.axis_index("gy")
     nx, ny = lax.axis_size("gx"), lax.axis_size("gy")
@@ -136,7 +138,11 @@
 
     load_classes = pltpu.make_async_copy(classes_hbm, classes, local_sem.at[0])
     load_ports = pltpu.make_async_copy(ports_hbm, ports, local_sem.at[1])
-    load_basis = pltpu.make_async_copy(basis2, q2, local_sem.at[2])
+    load_basis = pltpu.make_async_copy(
+        basis2.reshape(BLOCKS * COLS, rows, size_z),
+        q2.reshape(BLOCKS * COLS, pitch, size_z).at[:, pl.ds(0, rows), :],
+        local_sem.at[2],
+    )
     load_block = pltpu.make_async_copy(
         basis4.at[pl.ds(first, COLS)],
         pad.at[:, pl.ds(REACH, size_x), pl.ds(size_y, size_y), :],
@@ -285,8 +291,9 @@
 
     def split_block(c, carry):
         place = pl.ds(pl.multiple_of(c * rows, rows), rows)
+        image_place = pl.ds(pl.multiple_of(c * pitch, size_y), rows)
         own = pad[c, inner_x, inner_y, :]
-        w2[place, :] = (diag[...] * own).reshape(rows, size_z)
+        w2[image_place, :] = (diag[...] * own).reshape(rows, size_z)
         own = own.reshape(rows, size_z)
         high = own.astype(jnp.bfloat16).astype(jnp.float32)
         parts[place, :] = jnp.concatenate([high, own - high, high], axis=1).astype(jnp.bfloat16)
@@ -301,7 +308,7 @@
             lines = pl.ds(group * GROUP * rows, GROUP * rows)
             result = jnp.dot(parts[lines, :], bands[pair], preferred_element_type=jnp.float32)
             for i in range(GROUP):
-                place = pl.ds((group * GROUP + i) * rows, rows)
+                place = pl.ds((group * GROUP + i) * pitch, rows)
                 mine = result[i * rows : (i + 1) * rows]
                 w2[place, :] -= jnp.where(
                     even, mine[:, :size_z], jnp.where(odd, mine[:, size_z:], 0.0)
@@ -321,7 +328,7 @@
     def gather(ref, count, chunk):
         return jnp.concatenate(
             [
-                ref[pl.ds(chunk * per_chunk + i, count, stride=rows), :]
+                ref[pl.ds(chunk * per_chunk + i, count, stride=pitch), :]
                 for i in range(per_chunk)
             ],
             axis=1,
@@ -353,7 +360,7 @@
             def along(x, carry, axis=axis, group=group):
                 columns = range(group * GROUP, (group + 1) * GROUP)
                 places = [
-                    pl.ds(pl.multiple_of(c * rows + x * size_y, size_y), size_y) for c in columns
+                    pl.ds(pl.multiple_of(c * pitch + x * size_y, size_y), size_y) for c in columns
                 ]
                 images = [w2[place, :] for place in places]
                 for j in range(2 * REACH):
@@ -369,7 +376,7 @@
                     w2[place, :] = image
                 return carry
 
-            lax.fori_loop(0, size_x, along, 0)
+            lax.fori_loop(0, size_x, along, 0, unroll=2)
 
     exchange_x = Exchange("gx", qq_x, qq_x_send, qq_x_recv)
     exchange_x.start(exchange.finish())
@@ -436,7 +443,8 @@
     out_sem,
 ):
     chunks, _, span = halved.shape
-    rows, size_z = out2.shape[0] // COLS, out2.shape[1]
+    pitch, size_z = out2.shape[0] // COLS, out2.shape[1]
+    rows = pitch - PITCH
     per_chunk = span // size_z
     wide = BLOCKS * COLS
     sums = both_sums[:COLS, :] / total_cells
@@ -477,14 +485,14 @@
     def store(chunk):
         part = pl.ds(pl.multiple_of(chunk * per_chunk, per_chunk), per_chunk)
         return pltpu.make_async_copy(
-            out2.reshape(COLS, rows, size_z).at[:, part, :], out_hbm.at[:, part, :], out_sem.at[chunk]
+            out2.reshape(COLS, pitch, size_z).at[:, part, :], out_hbm.at[:, part, :], out_sem.at[chunk]
         )
 
     def combine(chunk, carry):
         result = jnp.dot(mix, halved[chunk], preferred_element_type=jnp.float32)
         result = result[:COLS] + result[COLS:]
         for i in range(per_chunk):
-            out2[pl.ds(chunk * per_chunk + i, COLS, stride=rows), :] = result[
+            out2[pl.ds(chunk * per_chunk + i, COLS, stride=pitch), :] = result[
                 :, i * size_z : (i + 1) * size_z
             ]
         store(chunk).start()
@@ -527,8 +535,8 @@
             pltpu.SMEM(taps.shape, jnp.float32),
             pltpu.SMEM(port_gain.shape, jnp.float32),
             vmem((COLS, size_x + 2 * REACH, 3 * size_y, size_z)),
-            vmem((wide * rows, size_z)),
-            vmem((COLS * rows, size_z)),
+            vmem((wide * (rows + PITCH), size_z)),
+            vmem((COLS * (rows + PITCH), size_z)),
             vmem((4 * REACH, size_x, size_y, size_z)),
             vmem((size_x, size_y, size_z)),
             pltpu.VMEM((MAT // 2, 3 * size_z, 2 * size_z), jnp.bfloat16),
@@ -577,7 +585,7 @@
         in_specs=[vmem_spec] * 2,
         out_specs=(hbm,) * 3,
         scratch_shapes=[
-            vmem((COLS * rows, size_z)),
+            vmem((COLS * (rows + PITCH), size_z)),
             vmem((COLS, wide)),
             vmem((COLS, COLS)),
             dma((2,)),

time: 28.8 us -> 28.2 us (0.979)
  Pallas kernels: 28 us -> 27.4 us
    pallas_call x1, Pallas kernels: 25.3 us -> 24.7 us  [per_device(): pl.pallas_call(functools.partial(gather_kernel, row_length), out_shape=(j...]
where the time goes in v7:
time: 28.2 us; the launch traced here: 28 us
  Pallas kernels  27.4 us (97%)
  between operations  0.64 us (2%)
    pallas_call x1, Pallas kernels, per_device(): pl.pallas_call(functools.partial(gather_kernel, row_length), out_shape=(j...  24.7 us
    pallas_call x1, Pallas kernels, per_device(): pl.pallas_call(functools.partial(combine_kernel, float(rows * size_z * nx...  2.75 us

profile of v7, /device:TPU:0, one launch (start us, length us, event | category | flops | bytes accessed | tf_op | source)
XLA Modules:
  0.0 28.0 jit_solution(14853821125037951641)
XLA Ops:
  0.6 24.7 %shard_map.76 = (bf16[8,80,2048]{2,1,0:T(8,128)(2,1)S(1)}, f32[40,128]{1,0:T(8,128)S(1)}) custom-call(f32[8,42]{1,0:T(8,128)} %taps_hbm.1, f32[8]{0:T(128)} %gain_hbm.1, f32[32,16,8,128]{3,2,1,0:T(8,128)} %basis4.1, f32[4096,128]{1,0:T(8,128)} %bitcast.3, s32[16,8,128]{2,1,0:T(8,128)} %classes_hbm.1, s32[16,8,128]{2,1,0:T(8,128)} %ports_hbm.1), custom_call_target="tpu_custom_call" | custom-call | tf_op jit(solution)/shard_map/pallas_call | solution.py:526
  25.3 2.7 %shard_map.77 = (f32[8,128,128]{2,1,0:T(8,128)}, f32[8,32]{1,0:T(8,128)}, f32[8,8]{1,0:T(8,128)}) custom-call(bf16[8,80,2048]{2,1,0:T(8,128)(2,1)S(1)} %get-tuple-element.8.halved, f32[40,128]{1,0:T(8,128)S(1)} %get-tuple-element.9.both_sums), custom_call_target="tpu_custom_call" | custom-call | tf_op jit(solution)/shard_map/pallas_call | solution.py:578

commit v8 on v7

--- a/solution.py
+++ b/solution.py
@@ -52,7 +52,7 @@
             self.copy(step, self.me, lax.rem(self.me + step, self.count)).start()
             return carry
 
-        lax.fori_loop(1, self.count, body, 0)
+        lax.fori_loop(1, self.count, body, 0, unroll=self.count <= 8)
 
     def finish(self):
         def body(step, carry):
@@ -60,7 +60,7 @@
             self.copy(step, peer, peer).wait_recv()
             return carry
 
-        lax.fori_loop(1, self.count, body, 0)
+        lax.fori_loop(1, self.count, body, 0, unroll=self.count <= 8)
         total = self.buf[0]
         for slot in range(1, self.count):
             total = total + self.buf[slot]
@@ -71,7 +71,7 @@
             self.copy(step, self.me, lax.rem(self.me + step, self.count)).wait_send()
             return carry
 
-        lax.fori_loop(1, self.count, body, 0)
+        lax.fori_loop(1, self.count, body, 0, unroll=self.count <= 8)
 
 
 def gather_kernel(
@@ -337,17 +337,17 @@
     def own_products(chunk, acc):
         both = halves(gather(q2, BLOCKS * COLS, chunk))
         halved[chunk, : 2 * wide, :] = both
-        return acc + lax.dot_general(both, both, NT, preferred_element_type=jnp.float32)
+        return acc + lax.dot_general(both, both[:wide], NT, preferred_element_type=jnp.float32)
 
     wide = BLOCKS * COLS
     acc = lax.fori_loop(
-        0, chunks, own_products, jnp.zeros((2 * wide, 2 * wide), jnp.float32), unroll=UNROLL
-    )
-    acc = acc[:wide] + acc[wide:]
-    local_qq = acc[:, :wide] + acc[:, wide:]
-    fill = jnp.zeros((wide, 128 - wide), jnp.float32)
+        0, chunks, own_products, jnp.zeros((2 * wide, wide), jnp.float32), unroll=UNROLL
+    )
+    local_qq = acc[:wide] + acc[wide:] + acc[wide:].T
     exchange = Exchange("gy", qq_y, qq_y_send, qq_y_recv)
-    exchange.start(jnp.concatenate([local_qq, fill], axis=1))
+    exchange.start(
+        jnp.concatenate([local_qq[i : i + COLS] for i in range(0, wide, COLS)], axis=1)
+    )
 
     for axis, first_way in (("gy", 0), ("gx", 2)):
         for group in range(COLS // GROUP):
@@ -405,28 +405,30 @@
     g_exchange = Exchange("gy", g_y, g_y_send, g_y_recv)
     g_exchange.start(local_g)
     sums[COLS:, :] = exchange_x.finish()
+    for group in range(COLS // GROUP):
+        for way in range(4):
+
+            @pl.when(sends(way, group))
+            def _(way=way, group=group):
+                halo(way, group).wait_send()
+
+    for direction, source, target, corner in turns:
+
+        @pl.when(gx == source)
+        def _(direction=direction, corner=corner):
+            to_corner(direction, corner).wait_send()
+
+        @pl.when(gx == corner)
+        def _(direction=direction, target=target):
+            from_corner(direction, target).wait_send()
+
+    exchange.drain()
+    exchange_x.drain()
     g_exchange_x = Exchange("gx", g_x, g_x_send, g_x_recv)
     g_exchange_x.start(g_exchange.finish())
     sums[:COLS, :] = g_exchange_x.finish()
-    for group in range(COLS // GROUP):
-        for way in range(4):
-
-            @pl.when(sends(way, group))
-            def _(way=way, group=group):
-                halo(way, group).wait_send()
-
-    for direction, source, target, corner in turns:
-
-        @pl.when(gx == source)
-        def _(direction=direction, corner=corner):
-            to_corner(direction, corner).wait_send()
-
-        @pl.when(gx == corner)
-        def _(direction=direction, target=target):
-            from_corner(direction, target).wait_send()
-
-    for each in (exchange, exchange_x, g_exchange, g_exchange_x):
-        each.drain()
+    g_exchange.drain()
+    g_exchange_x.drain()
 
 
 def combine_kernel(
@@ -448,12 +450,14 @@
     per_chunk = span // size_z
     wide = BLOCKS * COLS
     sums = both_sums[:COLS, :] / total_cells
-    sum_qq = both_sums[COLS:, :]
+    sum_qq = jnp.concatenate(
+        [both_sums[COLS:, i * wide : (i + 1) * wide] for i in range(BLOCKS)], axis=0
+    )
     proj_t = sums[:, :wide]
     proj_ref[...] = proj_t
     row = lax.broadcasted_iota(jnp.int32, (wide, wide), 0)
     column = lax.broadcasted_iota(jnp.int32, (wide, wide), 1)
-    middle = jnp.where(row == column, 2.0, 0.0) - sum_qq[:, :wide] / total_cells
+    middle = jnp.where(row == column, 2.0, 0.0) - sum_qq / total_cells
     left = jnp.dot(proj_t, middle, precision=HIGHEST, preferred_element_type=jnp.float32)
     gram = sums[:, wide : wide + COLS] - lax.dot_general(
         left, proj_t, NT, precision=HIGHEST, preferred_element_type=jnp.float32
@@ -522,7 +526,7 @@
     vmem_spec = pl.BlockSpec(memory_space=pltpu.VMEM)
     groups = COLS // GROUP
     halved_shape = (chunks, 2 * (wide + COLS), span)
-    sums_shape = (COLS + wide, 128)
+    sums_shape = (2 * COLS, BLOCKS * wide)
     halved, sums = pl.pallas_call(
         functools.partial(gather_kernel, row_length),
         out_shape=(
@@ -544,8 +548,8 @@
             pltpu.VMEM((size_x, size_y, size_z), jnp.int32),
             pltpu.VMEM((size_x, size_y, size_z), jnp.int32),
             vmem((2, GROUP, REACH, size_y, size_z)),
-            vmem((ny, wide, 128)),
-            vmem((nx, wide, 128)),
+            vmem((ny, COLS, BLOCKS * wide)),
+            vmem((nx, COLS, BLOCKS * wide)),
             vmem((ny, COLS, 128)),
             vmem((nx, COLS, 128)),
             dma((5,)),

time: 28.2 us -> 27.1 us (0.961)
  Pallas kernels: 27.4 us -> 26.3 us
    pallas_call x1, Pallas kernels: 24.7 us -> 23.5 us  [per_device(): pl.pallas_call(functools.partial(gather_kernel, row_length), out_shape=(j...]
where the time goes in v8:
time: 27.1 us; the launch traced here: 27 us
  Pallas kernels  26.3 us (97%)
  between operations  0.64 us (2%)
    pallas_call x1, Pallas kernels, per_device(): pl.pallas_call(functools.partial(gather_kernel, row_length), out_shape=(j...  23.5 us
    pallas_call x1, Pallas kernels, per_device(): pl.pallas_call(functools.partial(combine_kernel, float(rows * size_z * nx...  2.81 us

profile of v8, /device:TPU:0, one launch (start us, length us, event | category | flops | bytes accessed | tf_op | source)
XLA Modules:
  0.0 27.0 jit_solution(13200512440024505646)
XLA Ops:
  0.6 23.5 %shard_map.76 = (bf16[8,80,2048]{2,1,0:T(8,128)(2,1)S(1)}, f32[16,128]{1,0:T(8,128)S(1)}) custom-call(f32[8,42]{1,0:T(8,128)} %taps_hbm.1, f32[8]{0:T(128)} %gain_hbm.1, f32[32,16,8,128]{3,2,1,0:T(8,128)} %basis4.1, f32[4096,128]{1,0:T(8,128)} %bitcast.3, s32[16,8,128]{2,1,0:T(8,128)} %classes_hbm.1, s32[16,8,128]{2,1,0:T(8,128)} %ports_hbm.1), custom_call_target="tpu_custom_call" | custom-call | tf_op jit(solution)/shard_map/pallas_call | solution.py:530
  24.2 2.8 %shard_map.77 = (f32[8,128,128]{2,1,0:T(8,128)}, f32[8,32]{1,0:T(8,128)}, f32[8,8]{1,0:T(8,128)}) custom-call(bf16[8,80,2048]{2,1,0:T(8,128)(2,1)S(1)} %get-tuple-element.8.halved, f32[16,128]{1,0:T(8,128)S(1)} %get-tuple-element.9.both_sums), custom_call_target="tpu_custom_call" | custom-call | tf_op jit(solution)/shard_map/pallas_call | solution.py:582

commit v9 on v8

--- a/solution.py
+++ b/solution.py
@@ -381,18 +381,12 @@
     exchange_x = Exchange("gx", qq_x, qq_x_send, qq_x_recv)
     exchange_x.start(exchange.finish())
 
-    def image_products(chunk, acc):
+    acc = jnp.zeros((2 * (wide + COLS), 2 * COLS), jnp.float32)
+    for chunk in range(chunks):
         both = halves(gather(w2, COLS, chunk))
         halved[chunk, 2 * wide :, :] = both
-        return acc + lax.dot_general(halved[chunk], both, NT, preferred_element_type=jnp.float32)
-
-    acc = lax.fori_loop(
-        0,
-        chunks,
-        image_products,
-        jnp.zeros((2 * (wide + COLS), 2 * COLS), jnp.float32),
-        unroll=UNROLL,
-    )
+        all_rows = jnp.concatenate([halved[chunk, : 2 * wide, :], both], axis=0)
+        acc = acc + lax.dot_general(all_rows, both, NT, preferred_element_type=jnp.float32)
     acc = acc[:, :COLS] + acc[:, COLS:]
     local_g = jnp.concatenate(
         [
@@ -426,8 +420,8 @@
     exchange_x.drain()
     g_exchange_x = Exchange("gx", g_x, g_x_send, g_x_recv)
     g_exchange_x.start(g_exchange.finish())
+    g_exchange.drain()
     sums[:COLS, :] = g_exchange_x.finish()
-    g_exchange.drain()
     g_exchange_x.drain()
 
 
@@ -486,29 +480,25 @@
     mix_q, mix_w = mix[:, :wide], mix[:, wide:]
     mix = jnp.concatenate([mix_q, mix_q, mix_w, mix_w], axis=1).astype(jnp.bfloat16)
 
-    def store(chunk):
-        part = pl.ds(pl.multiple_of(chunk * per_chunk, per_chunk), per_chunk)
-        return pltpu.make_async_copy(
-            out2.reshape(COLS, pitch, size_z).at[:, part, :], out_hbm.at[:, part, :], out_sem.at[chunk]
+    pieces = 2 if chunks % 2 == 0 else 1
+    lines = rows // pieces
+    stores = []
+    for piece in range(pieces):
+        for chunk in range(piece * chunks // pieces, (piece + 1) * chunks // pieces):
+            result = jnp.dot(mix, halved[chunk], preferred_element_type=jnp.float32)
+            result = result[:COLS] + result[COLS:]
+            for i in range(per_chunk):
+                out2[pl.ds(chunk * per_chunk + i, COLS, stride=pitch), :] = result[
+                    :, i * size_z : (i + 1) * size_z
+                ]
+        part = pl.ds(piece * lines, lines)
+        store = pltpu.make_async_copy(
+            out2.reshape(COLS, pitch, size_z).at[:, part, :], out_hbm.at[:, part, :], out_sem.at[piece]
         )
-
-    def combine(chunk, carry):
-        result = jnp.dot(mix, halved[chunk], preferred_element_type=jnp.float32)
-        result = result[:COLS] + result[COLS:]
-        for i in range(per_chunk):
-            out2[pl.ds(chunk * per_chunk + i, COLS, stride=pitch), :] = result[
-                :, i * size_z : (i + 1) * size_z
-            ]
-        store(chunk).start()
-        return carry
-
-    lax.fori_loop(0, chunks, combine, 0, unroll=UNROLL)
-
-    def drain(chunk, carry):
-        store(chunk).wait()
-        return carry
-
-    lax.fori_loop(0, chunks, drain, 0)
+        store.start()
+        stores.append(store)
+    for store in stores:
+        store.wait()
     store_proj.wait()
     store_tri.wait()
 
@@ -593,7 +583,7 @@
             vmem((COLS, wide)),
             vmem((COLS, COLS)),
             dma((2,)),
-            dma((chunks,)),
+            dma((2,)),
         ],
         compiler_params=pltpu.CompilerParams(vmem_limit_bytes=24 * 1024 * 1024),
     )(halved, sums)

time: 27.1 us -> 26.8 us (0.989)
  no operation moved by 1% of the time
where the time goes in v9:
time: 26.8 us; the launch traced here: 26.7 us
  Pallas kernels  26.1 us (97%)
  between operations  0.64 us (2%)
    pallas_call x1, Pallas kernels, per_device(): pl.pallas_call(functools.partial(gather_kernel, row_length), out_shape=(j...  23.4 us
    pallas_call x1, Pallas kernels, per_device(): pl.pallas_call(functools.partial(combine_kernel, float(rows * size_z * nx...  2.69 us

profile of v9, /device:TPU:0, one launch (start us, length us, event | category | flops | bytes accessed | tf_op | source)
XLA Modules:
  0.0 26.7 jit_solution(18270103246988080141)
XLA Ops:
  0.6 23.4 %shard_map.76 = (bf16[8,80,2048]{2,1,0:T(8,128)(2,1)S(1)}, f32[16,128]{1,0:T(8,128)S(1)}) custom-call(f32[8,42]{1,0:T(8,128)} %taps_hbm.1, f32[8]{0:T(128)} %gain_hbm.1, f32[32,16,8,128]{3,2,1,0:T(8,128)} %basis4.1, f32[4096,128]{1,0:T(8,128)} %bitcast.3, s32[16,8,128]{2,1,0:T(8,128)} %classes_hbm.1, s32[16,8,128]{2,1,0:T(8,128)} %ports_hbm.1), custom_call_target="tpu_custom_call" | custom-call | tf_op jit(solution)/shard_map/pallas_call | solution.py:520
  24.0 2.7 %shard_map.77 = (f32[8,128,128]{2,1,0:T(8,128)}, f32[8,32]{1,0:T(8,128)}, f32[8,8]{1,0:T(8,128)}) custom-call(bf16[8,80,2048]{2,1,0:T(8,128)(2,1)S(1)} %get-tuple-element.8.halved, f32[16,128]{1,0:T(8,128)S(1)} %get-tuple-element.9.both_sums), custom_call_target="tpu_custom_call" | custom-call | tf_op jit(solution)/shard_map/pallas_call | solution.py:572

commit v10 on v9

--- a/solution.py
+++ b/solution.py
@@ -14,7 +14,6 @@
 PORTS = 8
 GROUP = 4
 LAYERS = 4
-UNROLL = 4
 PITCH = 8
 MESH = pl.DeviceIdType.MESH
 NT = (((1,), (1,)), ((), ()))
@@ -341,7 +340,7 @@
 
     wide = BLOCKS * COLS
     acc = lax.fori_loop(
-        0, chunks, own_products, jnp.zeros((2 * wide, wide), jnp.float32), unroll=UNROLL
+        0, chunks, own_products, jnp.zeros((2 * wide, wide), jnp.float32), unroll=True
     )
     local_qq = acc[:wide] + acc[wide:] + acc[wide:].T
     exchange = Exchange("gy", qq_y, qq_y_send, qq_y_recv)
@@ -376,7 +375,7 @@
                     w2[place, :] = image
                 return carry
 
-            lax.fori_loop(0, size_x, along, 0, unroll=2)
+            lax.fori_loop(0, size_x, along, 0, unroll=4)
 
     exchange_x = Exchange("gx", qq_x, qq_x_send, qq_x_recv)
     exchange_x.start(exchange.finish())

time: 26.8 us -> 27.5 us (1.026)
  Pallas kernels: 26.1 us -> 26.8 us
    pallas_call x1, Pallas kernels: 23.4 us -> 24.1 us  [per_device(): pl.pallas_call(functools.partial(gather_kernel, row_length), out_shape=(j...]
where the time goes in v10:
time: 27.5 us; the launch traced here: 27.4 us
  Pallas kernels  26.8 us (97%)
  between operations  0.64 us (2%)
    pallas_call x1, Pallas kernels, per_device(): pl.pallas_call(functools.partial(gather_kernel, row_length), out_shape=(j...  24.1 us
    pallas_call x1, Pallas kernels, per_device(): pl.pallas_call(functools.partial(combine_kernel, float(rows * size_z * nx...  2.69 us

profile of v10, /device:TPU:0, one launch (start us, length us, event | category | flops | bytes accessed | tf_op | source)
XLA Modules:
  0.0 27.4 jit_solution(4400236287046863786)
XLA Ops:
  0.6 24.1 %shard_map.76 = (bf16[8,80,2048]{2,1,0:T(8,128)(2,1)S(1)}, f32[16,128]{1,0:T(8,128)S(1)}) custom-call(f32[8,42]{1,0:T(8,128)} %taps_hbm.1, f32[8]{0:T(128)} %gain_hbm.1, f32[32,16,8,128]{3,2,1,0:T(8,128)} %basis4.1, f32[4096,128]{1,0:T(8,128)} %bitcast.3, s32[16,8,128]{2,1,0:T(8,128)} %classes_hbm.1, s32[16,8,128]{2,1,0:T(8,128)} %ports_hbm.1), custom_call_target="tpu_custom_call" | custom-call | tf_op jit(solution)/shard_map/pallas_call | solution.py:519
  24.7 2.7 %shard_map.77 = (f32[8,128,128]{2,1,0:T(8,128)}, f32[8,32]{1,0:T(8,128)}, f32[8,8]{1,0:T(8,128)}) custom-call(bf16[8,80,2048]{2,1,0:T(8,128)(2,1)S(1)} %get-tuple-element.8.halved, f32[16,128]{1,0:T(8,128)S(1)} %get-tuple-element.9.both_sums), custom_call_target="tpu_custom_call" | custom-call | tf_op jit(solution)/shard_map/pallas_call | solution.py:571
